TPU v7x, 512 devices: a whole 4x8x8 slice. The times are simulated.
512 devices in a mesh: seq: 64 (over y_lo, z, core), tp: 8 (over y_hi, x).
Axes of the slice: x: 4, y: 8 (y_hi: 2, y_lo: 4; y = y_hi * 4 + y_lo), z: 8, core: 2. Of those that a mesh axis runs over, the one named last changes fastest.
Arguments:
- queries: bfloat16 [8192, 16384], P('seq', 'tp'), may hold values from -64 to 64
- keys: bfloat16 [8192, 1024], P('seq', 'tp'), may hold values from -32 to 32
- values: bfloat16 [8192, 1024], P('seq', 'tp'), may hold values from -6 to 6
- block_start: int32 [64, 2], replicated, may hold values from 0 to 8128, as said below
Outputs:
- attended: bfloat16 [8192, 16384], P(('seq', 'tp'))
Inputs may be any that keep to these rules, and one draw needn't show every extreme that they name: `block_start`: the entries are the multiples of 64 below 8192, each exactly once: the document's half-blocks in a drawn order.
All inputs are finite; a program needn't handle non-finite values.
Results may differ from a plain program's by a relative error of at most 0.008.
Values may be sent and summed in bfloat16 or wider, within the bound.
No kernel may reach another device: no remote copies, remote signals or barrier semaphores. Data moves between devices by JAX's collectives and lax.ppermute only.
A program may use at most 64 MiB of HBM per device.

v0:
```python
import math

import jax
import jax.numpy as jnp
from jax import lax
from jax.experimental import pallas as pl
from jax.experimental.pallas import tpu as pltpu
from jax.sharding import PartitionSpec as P

HEAD_SIZE = 128
HALF_ROWS = 64
MASKED_SCORE = -1e30
COLUMN_CHIPS = 4
PLANE_DEVICES = 16
ROW_TILE = 256
KEY_CHUNK = 1024


def attend_kernel(place_ref, own_ref, query_ref, kv_ref, out_ref, scaled, total, largest):
    heads = query_ref.shape[1] // HEAD_SIZE
    half_height = heads * HALF_ROWS
    chunk_blocks = KEY_CHUNK // HALF_ROWS
    scale = math.log2(math.e) / math.sqrt(HEAD_SIZE)
    for half in range(2):
        for head in range(heads):
            part = query_ref[
                half * HALF_ROWS : (half + 1) * HALF_ROWS,
                head * HEAD_SIZE : (head + 1) * HEAD_SIZE,
            ]
            part = part.astype(jnp.float32) * scale
            high = part.astype(jnp.bfloat16)
            start = half * half_height + head * HALF_ROWS
            scaled[start : start + HALF_ROWS, :HEAD_SIZE] = high
            scaled[start : start + HALF_ROWS, HEAD_SIZE:] = (
                part - high.astype(jnp.float32)
            ).astype(jnp.bfloat16)
    total[...] = jnp.zeros_like(total)
    largest[...] = jnp.full_like(largest, MASKED_SCORE)
    ones = jnp.ones((KEY_CHUNK, HEAD_SIZE), jnp.bfloat16)

    def absorb(chunk, halves, masked):
        rows_of = [
            kv_ref[
                pl.ds(
                    pl.multiple_of(place_ref[chunk * chunk_blocks + i] * HALF_ROWS, HALF_ROWS),
                    HALF_ROWS,
                ),
                :,
            ]
            for i in range(chunk_blocks)
        ]
        kv = jnp.concatenate(rows_of, axis=0)
        keys = kv[:, :HEAD_SIZE]
        keys = jnp.concatenate([keys, keys], axis=1)
        values = jnp.concatenate([kv[:, HEAD_SIZE:], ones], axis=1)
        for half in halves:
            for tile in range(half_height // ROW_TILE):
                start = half * half_height + tile * ROW_TILE
                rows = slice(start, start + ROW_TILE)
                scores = lax.dot_general(
                    scaled[rows, :],
                    keys,
                    (((1,), (1,)), ((), ())),
                    preferred_element_type=jnp.float32,
                )
                if masked:
                    shape = (ROW_TILE, KEY_CHUNK)
                    row_pos = own_ref[half] + lax.rem(
                        lax.broadcasted_iota(jnp.int32, shape, 0), HALF_ROWS
                    )
                    key_pos = chunk * KEY_CHUNK + lax.broadcasted_iota(jnp.int32, shape, 1)
                    scores = jnp.where(key_pos <= row_pos, scores, MASKED_SCORE)
                old = largest[rows, :]
                new = jnp.maximum(old, jnp.max(scores, axis=1, keepdims=True))
                weights = jnp.exp2(scores - new[:, :1]).astype(jnp.bfloat16)
                fade = jnp.exp2(old - new)
                product = jnp.dot(weights, values, preferred_element_type=jnp.float32)
                total[rows, :] = total[rows, :] * jnp.concatenate([fade, fade], axis=1) + product
                largest[rows, :] = new

    def absorb_run(first, end, halves):
        def body(chunk, carry):
            absorb(chunk, halves, False)
            return carry

        lax.fori_loop(first, end, body, 0)

    last = [own_ref[half] // KEY_CHUNK for half in range(2)]
    shared = jnp.minimum(last[0], last[1])
    absorb_run(0, shared, (0, 1))
    for half in range(2):
        absorb_run(shared, last[half], (half,))
        absorb(last[half], (half,), True)
    for half in range(2):
        for head in range(heads):
            start = half * half_height + head * HALF_ROWS
            rows = slice(start, start + HALF_ROWS)
            out_ref[
                half * HALF_ROWS : (half + 1) * HALF_ROWS,
                head * HEAD_SIZE : (head + 1) * HEAD_SIZE,
            ] = (total[rows, :HEAD_SIZE] / total[rows, HEAD_SIZE:]).astype(jnp.bfloat16)


def attend(queries, kv, place, own_starts):
    row_count = queries.shape[0] * queries.shape[1] // HEAD_SIZE
    return pl.pallas_call(
        attend_kernel,
        out_shape=jax.ShapeDtypeStruct(queries.shape, jnp.bfloat16),
        in_specs=[pl.BlockSpec(memory_space=pltpu.SMEM)] * 2
        + [pl.BlockSpec(memory_space=pltpu.VMEM)] * 2,
        out_specs=pl.BlockSpec(memory_space=pltpu.VMEM),
        scratch_shapes=[
            pltpu.VMEM((row_count, 2 * HEAD_SIZE), jnp.bfloat16),
            pltpu.VMEM((row_count, 2 * HEAD_SIZE), jnp.float32),
            pltpu.VMEM((row_count, HEAD_SIZE), jnp.float32),
        ],
        compiler_params=pltpu.CompilerParams(vmem_limit_bytes=56 * 2**20),
        name="attend",
    )(place, own_starts, queries, kv)


def on_device(queries, keys, values, block_start):
    own_index = lax.axis_index("seq")
    columns = [
        [chip * PLANE_DEVICES + place for chip in range(COLUMN_CHIPS)]
        for place in range(PLANE_DEVICES)
    ]
    planes = [
        [chip * PLANE_DEVICES + place for place in range(PLANE_DEVICES)]
        for chip in range(COLUMN_CHIPS)
    ]
    kv = jnp.concatenate([keys, values], axis=1)
    kv = lax.all_gather(kv, "seq", axis=0, tiled=True, axis_index_groups=columns)
    kv = lax.all_gather(kv, "seq", axis=0, tiled=True, axis_index_groups=planes)
    order = block_start.reshape(COLUMN_CHIPS, PLANE_DEVICES, 2).transpose(1, 0, 2).reshape(-1)
    count = order.shape[0]
    at = jnp.arange(count, dtype=jnp.int32)
    place = jnp.sum(
        jnp.where(order[None, :] == at[:, None] * HALF_ROWS, at[None, :], 0), axis=1
    )
    own_starts = lax.dynamic_index_in_dim(block_start, own_index, 0, keepdims=False)
    attended = attend(queries, kv, place, own_starts)
    return lax.all_to_all(attended, "tp", split_axis=0, concat_axis=1, tiled=True)


def solution(mesh):
    placed = (P("seq", "tp"), P("seq", "tp"), P("seq", "tp"), P())
    return jax.shard_map(
        on_device, mesh=mesh, in_specs=placed, out_specs=P(("seq", "tp"), None), check_vma=False
    )
```

profile of v0, /device:TPU:208, one launch (start us, length us, event | category | flops | bytes accessed | tf_op | source)
XLA Modules:
  0.0 130.6 jit_solution(11415489180805327239)
XLA Ops:
  6.5 0.0 all-gather.2.cloned.1.call-start
  6.5 0.8 pad_maximum_fusion
  7.3 12.9 %all_gather.6 = bf16[512,256]{1,0:T(8,128)(2,1)} all-gather(bf16[128,256]{1,0:T(8,128)(2,1)S(1)} %pad_maximum_fusion), channel_id=1, replica_groups={{0,128,256,384},{8,136,264,392},{16,144,272,400},{24,152,280,408},{32,1..., dimensions={0}, use_global_device_ids=true | all-gather | bytes 327680 | tf_op jit(solution)/shard_map/all_gather | solution.py:133
  20.2 0.0 all-gather.2.cloned.1.call-update
  20.3 0.8 reshape.12
  21.0 1.5 %dynamic-slice_reduce_fusion.own_ref = s32[2]{0:T(128)} fusion(s32[64,2]{0,1:T(2,128)} %param.7, s32[]{:T(128)S(6)} %select_n.9), kind=kLoop, calls=%fused_computation.2 | loop fusion | bytes 20 | tf_op jit(solution)/shard_map/jit(dynamic_index_in_dim)/dynamic_slice | solution.py:141
  22.5 0.1 copy.9
  22.6 0.1 eq.15
  22.8 0.7 select_reduce_fusion.place_ref
  23.5 45.6 %all-gather.2.cloned.1.call-done.kv_ref = bf16[8192,256]{1,0:T(8,128)(2,1)} async-done(((bf16[512,256]{1,0:T(8,128)(2,1)}), bf16[8192,256]{1,0:T(8,128)(2,1)}) %all-gather.2.cloned.1.call-update) | async-done | bytes 4194320 | tf_op jit(solution)/shard_map/all_gather | solution.py:134
  69.0 27.0 %attend.1 = bf16[128,2048]{1,0:T(8,128)(2,1)} custom-call(s32[128]{0:T(128)} %select_reduce_fusion.place_ref, s32[2]{0:T(128)} %dynamic-slice_reduce_fusion.own_ref, bf16[128,2048]{1,0:T(8,128)(2,1)} %query_ref.1, bf16[8192,256]{1,0:T(8,128)(2,1)} %all-gather.2.cloned.1.call-done.kv_ref), custom_call_target="tpu_custom_call" | custom-call | tf_op jit(solution)/shard_map/attend/pallas_call | solution.py:106
  96.0 26.8 %all_to_all.19 = bf16[8,16,2048]{2,1,0:T(8,128)(2,1)S(1)} all-to-all(bf16[8,16,2048]{2,1,0:T(8,128)(2,1)} %bitcast.8), channel_id=1, replica_groups=mesh['seq'=64,'tp'=8] {'tp'}, dimensions={0} | all-to-all | bytes 1048576 | tf_op jit(solution)/shard_map/all_to_all | solution.py:143
  122.9 0.8 copy.11
  (1 shorter events, 0.0 us)
Async XLA Ops:
  6.5 62.5 %all-gather.2.cloned.1.call-start = ((), (), s32[]{:S(2)}) async-start(), calls=%async_computation.1 | async-start | bytes 4456448 | tf_op jit(solution)/shard_map/all_gather | solution.py:134
Sparse Core Ops, SparseCore 0:
  20.4 48.6 all-gather.1
where the time goes:
time: 131 us
  waiting for transfers between devices  45.6 us (35%)
  blocking collectives  39.8 us (30%)
  Pallas kernels  27 us (21%)
  between operations  13.4 us (10%)
  local copies, waits for them, and re-layouts  3.3 us (3%)
  other arithmetic  1.48 us (1%)
    all_gather x1, waiting for transfers between devices, on_device(): kv = lax.all_gather(kv, 'seq', axis=0, tiled=True, axis_index_groups=planes)  45.6 us
    pallas_call x1, Pallas kernels, attend(): pl.pallas_call(attend_kernel, out_shape=jax.ShapeDtypeStruct(queries.shap...  27 us
    all_to_all x1, blocking collectives, on_device(): lax.all_to_all(attended, 'tp', split_axis=0, concat_axis=1, tiled=True)  26.8 us
    all_gather x1, blocking collectives, on_device(): lax.all_gather(kv, 'seq', axis=0, tiled=True, axis_index_groups=columns)  12.9 us
  transfers between devices with their start and end apart: 1, of which 1 were waited for; matrix products, arithmetic and copies ran while one was open for 2% of the time, Pallas kernels for 0%

commit v1 on v0

v1 whole, which is shorter than its diff:
```python
import math

import jax
import jax.numpy as jnp
from jax import lax
from jax.experimental import pallas as pl
from jax.experimental.pallas import tpu as pltpu
from jax.sharding import PartitionSpec as P

HEAD_SIZE = 128
HALF_ROWS = 64
MASKED_SCORE = -1e30
ROW_TILE = 256
CHIPS_Y, CHIPS_Z, CORES = 4, 8, 2


def seq_index(y, z, core):
    return (y * CHIPS_Z + z % CHIPS_Z) * CORES + core


PLACES = [(y, z, core) for y in range(CHIPS_Y) for z in range(CHIPS_Z) for core in range(CORES)]
COLUMNS = [
    [seq_index(y, z, core) for y in range(CHIPS_Y) for core in range(CORES)]
    for z in range(CHIPS_Z)
]
ALONG_Z = [
    (seq_index(y, z, core), seq_index(y, z + 1 - 2 * core, core)) for y, z, core in PLACES
]
OTHER_CORE = [(seq_index(*place), seq_index(*place) ^ 1) for place in PLACES]


def absorb(scaled, unit, bias_of, total, largest):
    keys = unit[:, :HEAD_SIZE]
    keys = jnp.concatenate([keys, keys], axis=1)
    ones = jnp.ones((unit.shape[0], HEAD_SIZE), jnp.bfloat16)
    values = jnp.concatenate([unit[:, HEAD_SIZE:], ones], axis=1)
    count = scaled.shape[0] // ROW_TILE

    def scores_of(tile):
        return lax.dot_general(
            scaled[tile * ROW_TILE : (tile + 1) * ROW_TILE, :],
            keys,
            (((1,), (1,)), ((), ())),
            preferred_element_type=jnp.float32,
        )

    ahead = scores_of(0)
    for tile in range(count):
        rows = slice(tile * ROW_TILE, (tile + 1) * ROW_TILE)
        scores = bias_of(ahead, tile // (count // 2))
        if tile + 1 < count:
            ahead = scores_of(tile + 1)
        old = largest[rows, :]
        new = jnp.maximum(old, jnp.max(scores, axis=1, keepdims=True))
        weights = jnp.exp2(scores - new[:, :1]).astype(jnp.bfloat16)
        fade = jnp.exp2(old - new)
        product = jnp.dot(weights, values, preferred_element_type=jnp.float32)
        total[rows, :] = total[rows, :] * jnp.concatenate([fade, fade], axis=1) + product
        largest[rows, :] = new


def first_kernel(own_ref, query_ref, unit_ref, pos_ref, scaled, total, largest):
    heads = query_ref.shape[1] // HEAD_SIZE
    scale = math.log2(math.e) / math.sqrt(HEAD_SIZE)
    for half in range(2):
        for head in range(heads):
            part = query_ref[
                half * HALF_ROWS : (half + 1) * HALF_ROWS,
                head * HEAD_SIZE : (head + 1) * HEAD_SIZE,
            ]
            part = part.astype(jnp.float32) * scale
            high = part.astype(jnp.bfloat16)
            start = (half * heads + head) * HALF_ROWS
            scaled[start : start + HALF_ROWS, :HEAD_SIZE] = high
            scaled[start : start + HALF_ROWS, HEAD_SIZE:] = (
                part - high.astype(jnp.float32)
            ).astype(jnp.bfloat16)
    total[...] = jnp.zeros_like(total)
    largest[...] = jnp.full_like(largest, MASKED_SCORE)

    def masked(scores, half):
        row_pos = own_ref[half] + lax.rem(
            lax.broadcasted_iota(jnp.int32, scores.shape, 0), HALF_ROWS
        )
        return jnp.where(pos_ref[...] <= row_pos, scores, MASKED_SCORE)

    absorb(scaled, unit_ref[...], masked, total, largest)


def next_kernel(scaled, unit_ref, bias_ref, total_in, largest_in, total, largest):
    del total_in, largest_in

    def masked(scores, half):
        return scores + bias_ref[half : half + 1, :]

    absorb(scaled, unit_ref[...], masked, total, largest)


def last_kernel(scaled, near_ref, far_ref, bias_ref, total_in, largest_in, out_ref, total, largest):
    def masked(scores, half):
        return scores + bias_ref[half : half + 1, :]

    total[...] = total_in[...]
    largest[...] = largest_in[...]
    unit = jnp.concatenate([near_ref[...], far_ref[...]], axis=0)
    absorb(scaled, unit, masked, total, largest)
    heads = out_ref.shape[1] // HEAD_SIZE
    for half in range(2):
        for head in range(heads):
            start = (half * heads + head) * HALF_ROWS
            rows = slice(start, start + HALF_ROWS)
            out_ref[
                half * HALF_ROWS : (half + 1) * HALF_ROWS,
                head * HEAD_SIZE : (head + 1) * HEAD_SIZE,
            ] = (total[rows, :HEAD_SIZE] / total[rows, HEAD_SIZE:]).astype(jnp.bfloat16)


SMEM = pl.BlockSpec(memory_space=pltpu.SMEM)
VMEM = pl.BlockSpec(memory_space=pltpu.VMEM)
PARAMS = pltpu.CompilerParams(vmem_limit_bytes=40 * 2**20)


def after_kernel(value_ref, other_ref, out_ref):
    del value_ref, other_ref, out_ref


def after(value, other):
    anywhere = pl.BlockSpec(memory_space=pl.ANY)
    return pl.pallas_call(
        after_kernel,
        out_shape=jax.ShapeDtypeStruct(value.shape, value.dtype),
        in_specs=[anywhere] * 2,
        out_specs=anywhere,
        input_output_aliases={0: 0},
        name="after",
    )(value, other)


def kernel_cost(rows, keys):
    return pl.CostEstimate(
        flops=4 * rows * keys * 2 * HEAD_SIZE,
        bytes_accessed=2 * 2**20,
        transcendentals=rows * keys,
    )


def on_device(queries, keys, values, block_start):
    own_index = lax.axis_index("seq")
    core = own_index % CORES
    own_z = (own_index // CORES) % CHIPS_Z
    row_count = queries.shape[0] * queries.shape[1] // HEAD_SIZE

    kv = jnp.concatenate([keys, values], axis=1)
    own_unit = lax.all_gather(kv, "seq", axis=0, tiled=True, axis_index_groups=COLUMNS)
    unit_rows = own_unit.shape[0]

    starts = block_start.reshape(CHIPS_Y, CHIPS_Z, CORES * 2).transpose(1, 0, 2)
    starts = starts.reshape(CHIPS_Z, -1)
    starts = jnp.concatenate([starts, starts], axis=0)
    starts = lax.dynamic_slice_in_dim(starts, own_z, CHIPS_Z, 0)
    own_starts = lax.dynamic_index_in_dim(block_start, own_index, 0, keepdims=False)
    positions = jnp.repeat(starts, HALF_ROWS, axis=1)
    own_pos = positions[:1] + lax.rem(
        lax.broadcasted_iota(jnp.int32, (1, unit_rows), 1), HALF_ROWS
    )
    bias = jnp.where(
        positions[:, None, :] < own_starts[None, :, None], 0.0, MASKED_SCORE
    ).astype(jnp.float32)

    def shape(rows, columns, dtype):
        return jax.ShapeDtypeStruct((rows, columns), dtype)

    state = [
        shape(row_count, 2 * HEAD_SIZE, jnp.float32),
        shape(row_count, HEAD_SIZE, jnp.float32),
    ]
    scaled, total, largest = pl.pallas_call(
        first_kernel,
        out_shape=[shape(row_count, 2 * HEAD_SIZE, jnp.bfloat16)] + state,
        in_specs=[SMEM] + [VMEM] * 3,
        out_specs=[VMEM] * 3,
        compiler_params=PARAMS,
        cost_estimate=kernel_cost(row_count, unit_rows),
        name="attend_first",
    )(own_starts, queries, own_unit, own_pos)

    def attend_next(unit, bias, total, largest):
        return pl.pallas_call(
            next_kernel,
            out_shape=state,
            in_specs=[VMEM] * 5,
            out_specs=[VMEM] * 2,
            input_output_aliases={3: 0, 4: 1},
            compiler_params=PARAMS,
            cost_estimate=kernel_cost(row_count, unit_rows),
            name="attend_next",
        )(scaled, unit, bias, total, largest)

    unit = lax.ppermute(own_unit, "seq", ALONG_Z)
    for step in range(1, CHIPS_Z // 2):
        unit = after(unit, largest)
        here = unit
        if step + 1 == CHIPS_Z // 2:
            unit = lax.dynamic_slice_in_dim(unit, core * (unit_rows // 2), unit_rows // 2, 0)
        unit = lax.ppermute(unit, "seq", ALONG_Z)
        other = lax.ppermute(here, "seq", OTHER_CORE)
        lower, upper = bias[CHIPS_Z - step], bias[step]
        total, largest = attend_next(
            here, jnp.where(core == 0, lower, upper), total, largest
        )
        halfway = largest
        total, largest = attend_next(
            other, jnp.where(core == 0, upper, lower), total, largest
        )
    unit = after(unit, halfway)
    other = lax.ppermute(unit, "seq", OTHER_CORE)
    opposite = bias[CHIPS_Z // 2]
    opposite = jnp.where(core == 0, opposite, jnp.roll(opposite, unit_rows // 2, axis=1))
    attended = pl.pallas_call(
        last_kernel,
        out_shape=shape(queries.shape[0], queries.shape[1], jnp.bfloat16),
        in_specs=[VMEM] * 6,
        out_specs=VMEM,
        scratch_shapes=[
            pltpu.VMEM((row_count, 2 * HEAD_SIZE), jnp.float32),
            pltpu.VMEM((row_count, HEAD_SIZE), jnp.float32),
        ],
        compiler_params=PARAMS,
        cost_estimate=kernel_cost(row_count, unit_rows),
        name="attend_last",
    )(scaled, unit, other, opposite, total, largest)
    return lax.all_to_all(attended, "tp", split_axis=0, concat_axis=1, tiled=True)


def solution(mesh):
    placed = (P("seq", "tp"), P("seq", "tp"), P("seq", "tp"), P())
    return jax.shard_map(
        on_device, mesh=mesh, in_specs=placed, out_specs=P(("seq", "tp"), None), check_vma=False
    )
```

time: 131 us -> 131 us (level)
  the two profiles are of different devices: /device:TPU:208 before, /device:TPU:16 now
where the time goes in v1:
time: 131 us; the launch traced here: 130 us
  blocking collectives  47.5 us (36%)
  local copies, waits for them, and re-layouts  31.3 us (24%)
  Pallas kernels  26.4 us (20%)
  starting transfers between devices  21.7 us (17%)
  waiting for transfers between devices  1.48 us (1%)
    all_to_all x1, blocking collectives, on_device(): lax.all_to_all(attended, 'tp', split_axis=0, concat_axis=1, tiled=True)  29 us
    unnamed x55, local copies, waits for them, and re-layouts  27.9 us
    pallas_call x6, Pallas kernels, attend_next(): pl.pallas_call(next_kernel, out_shape=state, in_specs=[VMEM] * 5, out_spe...  19.5 us
    all_gather x1, blocking collectives, on_device(): lax.all_gather(kv, 'seq', axis=0, tiled=True, axis_index_groups=COLUMNS)  18.5 us
    ppermute x3, starting transfers between devices, on_device(): other = lax.ppermute(here, 'seq', OTHER_CORE)  10 us
    ppermute x3, starting transfers between devices, on_device(): unit = lax.ppermute(unit, 'seq', ALONG_Z)  7.41 us
    pallas_call x1, Pallas kernels, on_device(): pl.pallas_call(first_kernel, out_shape=[shape(row_count, 2 * HEAD_SIZE, j...  3.6 us
    pallas_call x1, Pallas kernels, on_device(): pl.pallas_call(last_kernel, out_shape=shape(queries.shape[0], queries.sha...  3.28 us
  transfers between devices with their start and end apart: 8, of which 1 were waited for; matrix products, arithmetic and copies ran while one was open for 3% of the time, Pallas kernels for 18%

profile of v1, /device:TPU:16, one launch (start us, length us, event | category | flops | bytes accessed | tf_op | source)
XLA Modules:
  0.0 129.7 jit_solution(11791957478473620932)
XLA Ops:
  0.0 0.8 pad_maximum_fusion
  0.8 18.5 %all_gather.3.unit_ref = bf16[1024,256]{1,0:T(8,128)(2,1)S(1)} all-gather(bf16[128,256]{1,0:T(8,128)(2,1)S(1)} %pad_maximum_fusion), channel_id=1, replica_groups={{0,8,128,136,256,264,384,392},{16,24,144,152,272,280,400,408},{32,40,16..., dimensions={0}, use_global_device_ids=true | all-gather | bytes 589824 | tf_op jit(solution)/shard_map/all_gather | solution.py:154
  19.2 1.9 %collective-permute-start = (bf16[1024,256]{1,0:T(8,128)(2,1)S(1)}, bf16[1024,256]{1,0:T(8,128)(2,1)S(1)}, u32[]{:S(2)}, u32[]{:S(2)}) collective-permute-start(bf16[1024,256]{1,0:T(8,128)(2,1)S(1)} %all_gather.3.unit_ref), channel_id=1, source_target_pairs={{0,16},{8,120},{16,32},{24,8},{32,48},{40,24},{48,64},{56,40},{64,... | collective-permute-start | bytes 1572872 | tf_op jit(solution)/shard_map/ppermute | solution.py:199
  21.2 0.8 copy.25
  22.0 0.9 dynamic-slice_reduce_fusion.own_ref
  22.8 0.1 reshape.57
  22.9 0.1 copy.26
  23.0 0.1 dynamic-slice_add_fusion
  23.1 0.1 copy.27
  23.1 0.1 slice_reduce_fusion
  23.3 0.1 broadcast_in_dim.16
  23.3 0.1 broadcast_in_dim.17
  23.4 0.1 broadcast_in_dim.18
  23.5 0.1 lt.39
  23.6 0.0 copy-start.16
  23.6 1.0 copy-done.16
  24.6 3.6 %attend_first.1 = (bf16[2048,256]{1,0:T(8,128)(2,1)S(1)}, f32[2048,256]{1,0:T(8,128)S(1)}, f32[2048,128]{1,0:T(8,128)S(1)}) custom-call(s32[2]{0:T(128)S(1)} %dynamic-slice_reduce_fusion.own_ref, bf16[128,2048]{1,0:T(8,128)(2,1)S(1)} %copy-done.16, bf16[1024,256]{1,0:T(8,128)(2,1)S(1)} %all_gather.3.unit_ref, s32[1,1024]{1,0:T(1,128)S(1)} %and_add_fusion.pos_ref), custom_call_target="tpu_custom_call" | custom-call | flops 2147483648 | bytes 2097152 | tf_op jit(solution)/shard_map/attend_first/pallas_call | solution.py:177
  28.3 1.0 copy-done
  29.2 1.4 %copy-done.17 = f32[2048,256]{1,0:T(8,128)} copy-done((f32[2048,256]{1,0:T(8,128)}, f32[2048,256]{1,0:T(8,128)S(1)}, u32[]{:S(2)}) %copy-start.17) | copy-done | bytes 2097176
  30.6 1.5 %collective-permute-done.value_ref = bf16[1024,256]{1,0:T(8,128)(2,1)S(1)} collective-permute-done((bf16[1024,256]{1,0:T(8,128)(2,1)S(1)}, bf16[1024,256]{1,0:T(8,128)(2,1)S(1)}, u32[]{:S(2)}, u32[]{:S(2)}) %collective-permute-start) | collective-permute-done | bytes 524320 | tf_op jit(solution)/shard_map/ppermute | solution.py:199
  32.1 0.8 copy-done.10
  32.9 4.3 %collective-permute-start.2 = (bf16[1024,256]{1,0:T(8,128)(2,1)}, bf16[1024,256]{1,0:T(8,128)(2,1)S(1)}, u32[]{:S(2)}, u32[]{:S(2)}) collective-permute-start(bf16[1024,256]{1,0:T(8,128)(2,1)} %after.4.unit_ref), channel_id=1, source_target_pairs={{0,8},{8,0},{16,24},{24,16},{32,40},{40,32},{48,56},{56,48},{64,72... | collective-permute-start | bytes 1572872 | tf_op jit(solution)/shard_map/ppermute | solution.py:206
  37.1 0.1 compare_select_fusion
  37.3 1.9 %collective-permute-start.1 = (bf16[1024,256]{1,0:T(8,128)(2,1)}, bf16[1024,256]{1,0:T(8,128)(2,1)S(1)}, u32[]{:S(2)}, u32[]{:S(2)}) collective-permute-start(bf16[1024,256]{1,0:T(8,128)(2,1)} %after.4.unit_ref), channel_id=1, source_target_pairs={{0,16},{8,120},{16,32},{24,8},{32,48},{40,24},{48,64},{56,40},{64,... | collective-permute-start | bytes 1572872 | tf_op jit(solution)/shard_map/ppermute | solution.py:205
  39.2 0.0 copy-start.11
  39.2 1.0 copy-done.11
  40.3 1.6 %copy-done.18 = f32[2048,256]{1,0:T(8,128)S(1)} copy-done((f32[2048,256]{1,0:T(8,128)S(1)}, f32[2048,256]{1,0:T(8,128)}, u32[]{:S(2)}) %copy-start.18) | copy-done | bytes 2097176
  41.9 3.2 %attend_next.6 = (f32[2048,256]{1,0:T(8,128)S(1)}, f32[2048,128]{1,0:T(8,128)S(1)}) custom-call(bf16[2048,256]{1,0:T(8,128)(2,1)S(1)} %get-tuple-element.20.scaled, bf16[1024,256]{1,0:T(8,128)(2,1)S(1)} %copy-done.11, f32[2,1024]{1,0:T(2,128)S(1)} %get-tuple-element.37.bias_ref, ...), custom_call_target="tpu_custom_call", output_to_operand_aliasing={{0}: (3, {}), {1}: (4, {})} | custom-call | flops 2147483648 | bytes 2097152 | tf_op jit(solution)/shard_map/attend_next/pallas_call | solution.py:188
  45.1 0.0 collective-permute-done.2.unit_ref
  45.1 3.3 %attend_next.7 = (f32[2048,256]{1,0:T(8,128)S(1)}, f32[2048,128]{1,0:T(8,128)S(1)}) custom-call(bf16[2048,256]{1,0:T(8,128)(2,1)S(1)} %get-tuple-element.20.scaled, bf16[1024,256]{1,0:T(8,128)(2,1)S(1)} %collective-permute-done.2.unit_ref, f32[2,1024]{1,0:T(2,128)S(1)} %get-tuple-element.41.bias_ref, ...), custom_call_target="tpu_custom_call", output_to_operand_aliasing={{0}: (3, {}), {1}: (4, {})} | custom-call | flops 2147483648 | bytes 2097152 | tf_op jit(solution)/shard_map/attend_next/pallas_call | solution.py:188
  48.4 1.0 copy-done.2
  49.4 1.4 %copy-done.19 = f32[2048,256]{1,0:T(8,128)} copy-done((f32[2048,256]{1,0:T(8,128)}, f32[2048,256]{1,0:T(8,128)S(1)}, u32[]{:S(2)}) %copy-start.19) | copy-done | bytes 2097176
  50.7 0.0 collective-permute-done.1.value_ref
  50.7 0.8 copy-done.12
  51.5 2.2 %collective-permute-start.4 = (bf16[1024,256]{1,0:T(8,128)(2,1)}, bf16[1024,256]{1,0:T(8,128)(2,1)S(1)}, u32[]{:S(2)}, u32[]{:S(2)}) collective-permute-start(bf16[1024,256]{1,0:T(8,128)(2,1)} %after.5.unit_ref), channel_id=1, source_target_pairs={{0,8},{8,0},{16,24},{24,16},{32,40},{40,32},{48,56},{56,48},{64,72... | collective-permute-start | bytes 1572872 | tf_op jit(solution)/shard_map/ppermute | solution.py:206
  53.7 3.6 %collective-permute-start.3 = (bf16[1024,256]{1,0:T(8,128)(2,1)}, bf16[1024,256]{1,0:T(8,128)(2,1)S(1)}, u32[]{:S(2)}, u32[]{:S(2)}) collective-permute-start(bf16[1024,256]{1,0:T(8,128)(2,1)} %after.5.unit_ref), channel_id=1, source_target_pairs={{0,16},{8,120},{16,32},{24,8},{32,48},{40,24},{48,64},{56,40},{64,... | collective-permute-start | bytes 1572872 | tf_op jit(solution)/shard_map/ppermute | solution.py:205
  57.3 0.0 copy-start.13
  57.3 1.0 copy-done.13
  58.3 1.6 %copy-done.20 = f32[2048,256]{1,0:T(8,128)S(1)} copy-done((f32[2048,256]{1,0:T(8,128)S(1)}, f32[2048,256]{1,0:T(8,128)}, u32[]{:S(2)}) %copy-start.20) | copy-done | bytes 2097176
  59.9 3.3 %attend_next.8 = (f32[2048,256]{1,0:T(8,128)S(1)}, f32[2048,128]{1,0:T(8,128)S(1)}) custom-call(bf16[2048,256]{1,0:T(8,128)(2,1)S(1)} %get-tuple-element.20.scaled, bf16[1024,256]{1,0:T(8,128)(2,1)S(1)} %copy-done.13, f32[2,1024]{1,0:T(2,128)S(1)} %get-tuple-element.39.bias_ref, ...), custom_call_target="tpu_custom_call", output_to_operand_aliasing={{0}: (3, {}), {1}: (4, {})} | custom-call | flops 2147483648 | bytes 2097152 | tf_op jit(solution)/shard_map/attend_next/pallas_call | solution.py:188
  63.2 3.2 %attend_next.9 = (f32[2048,256]{1,0:T(8,128)S(1)}, f32[2048,128]{1,0:T(8,128)S(1)}) custom-call(bf16[2048,256]{1,0:T(8,128)(2,1)S(1)} %get-tuple-element.20.scaled, bf16[1024,256]{1,0:T(8,128)(2,1)S(1)} %collective-permute-done.4.unit_ref, f32[2,1024]{1,0:T(2,128)S(1)} %get-tuple-element.38.bias_ref, ...), custom_call_target="tpu_custom_call", output_to_operand_aliasing={{0}: (3, {}), {1}: (4, {})} | custom-call | flops 2147483648 | bytes 2097152 | tf_op jit(solution)/shard_map/attend_next/pallas_call | solution.py:188
  66.5 1.0 copy-done.4
  67.4 1.4 %copy-done.21 = f32[2048,256]{1,0:T(8,128)} copy-done((f32[2048,256]{1,0:T(8,128)}, f32[2048,256]{1,0:T(8,128)S(1)}, u32[]{:S(2)}) %copy-start.21) | copy-done | bytes 2097176
  68.8 0.8 copy-done.8
  69.6 3.6 %collective-permute-start.7 = (bf16[1024,256]{1,0:T(8,128)(2,1)}, bf16[1024,256]{1,0:T(8,128)(2,1)S(1)}, u32[]{:S(2)}, u32[]{:S(2)}) collective-permute-start(bf16[1024,256]{1,0:T(8,128)(2,1)} %after.6.unit_ref), channel_id=1, source_target_pairs={{0,8},{8,0},{16,24},{24,16},{32,40},{40,32},{48,56},{56,48},{64,72... | collective-permute-start | bytes 1572872 | tf_op jit(solution)/shard_map/ppermute | solution.py:206
  73.2 1.0 constant_dynamic-slice_fusion
  74.2 1.9 %collective-permute-start.5 = (bf16[512,256]{1,0:T(8,128)(2,1)S(1)}, bf16[512,256]{1,0:T(8,128)(2,1)S(1)}, u32[]{:S(2)}, u32[]{:S(2)}) collective-permute-start(bf16[512,256]{1,0:T(8,128)(2,1)S(1)} %constant_dynamic-slice_fusion), channel_id=1, source_target_pairs={{0,16},{8,120},{16,32},{24,8},{32,48},{40,24},{48,64},{56,40},{64,... | collective-permute-start | bytes 786440 | tf_op jit(solution)/shard_map/ppermute | solution.py:205
  76.1 0.0 copy-start.9
  76.2 1.0 copy-done.9
  77.2 1.6 %copy-done.22 = f32[2048,256]{1,0:T(8,128)S(1)} copy-done((f32[2048,256]{1,0:T(8,128)S(1)}, f32[2048,256]{1,0:T(8,128)}, u32[]{:S(2)}) %copy-start.22) | copy-done | bytes 2097176
  78.8 3.3 %attend_next.10 = (f32[2048,256]{1,0:T(8,128)S(1)}, f32[2048,128]{1,0:T(8,128)S(1)}) custom-call(bf16[2048,256]{1,0:T(8,128)(2,1)S(1)} %get-tuple-element.20.scaled, bf16[1024,256]{1,0:T(8,128)(2,1)S(1)} %copy-done.9, f32[2,1024]{1,0:T(2,128)S(1)} %get-tuple-element.40.bias_ref, ...), custom_call_target="tpu_custom_call", output_to_operand_aliasing={{0}: (3, {}), {1}: (4, {})} | custom-call | flops 2147483648 | bytes 2097152 | tf_op jit(solution)/shard_map/attend_next/pallas_call | solution.py:188
  82.0 1.0 copy-done.6
  83.0 1.4 %copy-done.23 = f32[2048,256]{1,0:T(8,128)} copy-done((f32[2048,256]{1,0:T(8,128)}, f32[2048,256]{1,0:T(8,128)S(1)}, u32[]{:S(2)}) %copy-start.23) | copy-done | bytes 2097176
  84.4 0.7 copy-done.14
  85.1 2.4 %collective-permute-start.6 = (bf16[512,256]{1,0:T(8,128)(2,1)}, bf16[512,256]{1,0:T(8,128)(2,1)S(1)}, u32[]{:S(2)}, u32[]{:S(2)}) collective-permute-start(bf16[512,256]{1,0:T(8,128)(2,1)} %after.7.near_ref), channel_id=1, source_target_pairs={{0,8},{8,0},{16,24},{24,16},{32,40},{40,32},{48,56},{56,48},{64,72... | collective-permute-start | bytes 786440 | tf_op jit(solution)/shard_map/ppermute | solution.py:216
  87.5 1.2 copy-done.7
  88.8 1.6 %copy-done.24 = f32[2048,256]{1,0:T(8,128)S(1)} copy-done((f32[2048,256]{1,0:T(8,128)S(1)}, f32[2048,256]{1,0:T(8,128)}, u32[]{:S(2)}) %copy-start.24) | copy-done | bytes 2097176
  90.3 3.2 %attend_next.11 = (f32[2048,256]{1,0:T(8,128)S(1)}, f32[2048,128]{1,0:T(8,128)S(1)}) custom-call(bf16[2048,256]{1,0:T(8,128)(2,1)S(1)} %get-tuple-element.20.scaled, bf16[1024,256]{1,0:T(8,128)(2,1)S(1)} %collective-permute-done.7.unit_ref, f32[2,1024]{1,0:T(2,128)S(1)} %get-tuple-element.35.bias_ref, ...), custom_call_target="tpu_custom_call", output_to_operand_aliasing={{0}: (3, {}), {1}: (4, {})} | custom-call | flops 2147483648 | bytes 2097152 | tf_op jit(solution)/shard_map/attend_next/pallas_call | solution.py:188
  93.6 1.4 %copy-done.25 = f32[2048,256]{1,0:T(8,128)} copy-done((f32[2048,256]{1,0:T(8,128)}, f32[2048,256]{1,0:T(8,128)S(1)}, u32[]{:S(2)}) %copy-start.25) | copy-done | bytes 2097176
  95.0 0.0 collective-permute-done.6.far_ref
  95.0 1.6 %copy-done.26 = f32[2048,256]{1,0:T(8,128)S(1)} copy-done((f32[2048,256]{1,0:T(8,128)S(1)}, f32[2048,256]{1,0:T(8,128)}, u32[]{:S(2)}) %copy-start.26) | copy-done | bytes 2097176
  96.6 3.3 %attend_last.1 = bf16[128,2048]{1,0:T(8,128)(2,1)S(1)} custom-call(bf16[2048,256]{1,0:T(8,128)(2,1)S(1)} %get-tuple-element.20.scaled, bf16[512,256]{1,0:T(8,128)(2,1)S(1)} %copy-done.15, bf16[512,256]{1,0:T(8,128)(2,1)S(1)} %collective-permute-done.6.far_ref, f32[2,1024]{1,0:T(2,128)S(1)} %maximum_select_fusion.bias_ref, f32[2048,256]{1,0:T(8,128)S(1)} %copy-done.26, ...), custom_call_target="tpu_custom_call" | custom-call | flops 2147483648 | bytes 2097152 | tf_op jit(solution)/shard_map/attend_last/pallas_call | solution.py:219
  99.8 29.0 %all_to_all.19 = bf16[8,16,2048]{2,1,0:T(8,128)(2,1)S(1)} all-to-all(bf16[8,16,2048]{2,1,0:T(8,128)(2,1)S(1)} %bitcast.22), channel_id=1, replica_groups=mesh['seq'=64,'tp'=8] {'tp'}, dimensions={0} | all-to-all | bytes 1048576 | tf_op jit(solution)/shard_map/all_to_all | solution.py:232
  128.9 0.8 copy.29
  (39 shorter events, 0.1 us)
Async XLA Ops:
  19.2 12.8 %collective-permute-start = (bf16[1024,256]{1,0:T(8,128)(2,1)S(1)}, bf16[1024,256]{1,0:T(8,128)(2,1)S(1)}, u32[]{:S(2)}, u32[]{:S(2)}) collective-permute-start(bf16[1024,256]{1,0:T(8,128)(2,1)S(1)} %all_gather.3.unit_ref), channel_id=1, source_target_pairs={{0,16},{8,120},{16,32},{24,8},{32,48},{40,24},{48,64},{56,40},{64,... | collective-permute-start | bytes 1572872 | tf_op jit(solution)/shard_map/ppermute | solution.py:199
  23.6 1.0 copy-start.16
  28.3 1.0 copy-start
  29.2 1.4 %copy-start.17 = (f32[2048,256]{1,0:T(8,128)}, f32[2048,256]{1,0:T(8,128)S(1)}, u32[]{:S(2)}) copy-start(f32[2048,256]{1,0:T(8,128)S(1)} %get-tuple-element.22.total_in) | copy-start | bytes 6291460
  32.1 0.8 copy-start.10
  32.1 7.1 %copy-start.1 = (f32[2048,128]{1,0:T(8,128)S(1)}, f32[2048,128]{1,0:T(8,128)}, u32[]{:S(2)}) copy-start(f32[2048,128]{1,0:T(8,128)} %copy-done) | copy-start | bytes 3145732
  32.9 12.2 %collective-permute-start.2 = (bf16[1024,256]{1,0:T(8,128)(2,1)}, bf16[1024,256]{1,0:T(8,128)(2,1)S(1)}, u32[]{:S(2)}, u32[]{:S(2)}) collective-permute-start(bf16[1024,256]{1,0:T(8,128)(2,1)} %after.4.unit_ref), channel_id=1, source_target_pairs={{0,8},{8,0},{16,24},{24,16},{32,40},{40,32},{48,56},{56,48},{64,72... | collective-permute-start | bytes 1572872 | tf_op jit(solution)/shard_map/ppermute | solution.py:206
  37.3 13.5 %collective-permute-start.1 = (bf16[1024,256]{1,0:T(8,128)(2,1)}, bf16[1024,256]{1,0:T(8,128)(2,1)S(1)}, u32[]{:S(2)}, u32[]{:S(2)}) collective-permute-start(bf16[1024,256]{1,0:T(8,128)(2,1)} %after.4.unit_ref), channel_id=1, source_target_pairs={{0,16},{8,120},{16,32},{24,8},{32,48},{40,24},{48,64},{56,40},{64,... | collective-permute-start | bytes 1572872 | tf_op jit(solution)/shard_map/ppermute | solution.py:205
  39.2 1.1 copy-start.11
  40.3 1.6 %copy-start.18 = (f32[2048,256]{1,0:T(8,128)S(1)}, f32[2048,256]{1,0:T(8,128)}, u32[]{:S(2)}) copy-start(f32[2048,256]{1,0:T(8,128)} %copy-done.17) | copy-start | bytes 6291460
  48.4 1.0 copy-start.2
  49.4 1.4 %copy-start.19 = (f32[2048,256]{1,0:T(8,128)}, f32[2048,256]{1,0:T(8,128)S(1)}, u32[]{:S(2)}) copy-start(f32[2048,256]{1,0:T(8,128)S(1)} %get-tuple-element.26.total_in) | copy-start | bytes 6291460
  50.7 0.8 copy-start.12
  50.7 6.5 %copy-start.3 = (f32[2048,128]{1,0:T(8,128)S(1)}, f32[2048,128]{1,0:T(8,128)}, u32[]{:S(2)}) copy-start(f32[2048,128]{1,0:T(8,128)} %copy-done.2) | copy-start | bytes 3145732
  51.5 11.7 %collective-permute-start.4 = (bf16[1024,256]{1,0:T(8,128)(2,1)}, bf16[1024,256]{1,0:T(8,128)(2,1)S(1)}, u32[]{:S(2)}, u32[]{:S(2)}) collective-permute-start(bf16[1024,256]{1,0:T(8,128)(2,1)} %after.5.unit_ref), channel_id=1, source_target_pairs={{0,8},{8,0},{16,24},{24,16},{32,40},{40,32},{48,56},{56,48},{64,72... | collective-permute-start | bytes 1572872 | tf_op jit(solution)/shard_map/ppermute | solution.py:206
  53.7 15.1 %collective-permute-start.3 = (bf16[1024,256]{1,0:T(8,128)(2,1)}, bf16[1024,256]{1,0:T(8,128)(2,1)S(1)}, u32[]{:S(2)}, u32[]{:S(2)}) collective-permute-start(bf16[1024,256]{1,0:T(8,128)(2,1)} %after.5.unit_ref), channel_id=1, source_target_pairs={{0,16},{8,120},{16,32},{24,8},{32,48},{40,24},{48,64},{56,40},{64,... | collective-permute-start | bytes 1572872 | tf_op jit(solution)/shard_map/ppermute | solution.py:205
  57.3 1.0 copy-start.13
  58.3 1.6 %copy-start.20 = (f32[2048,256]{1,0:T(8,128)S(1)}, f32[2048,256]{1,0:T(8,128)}, u32[]{:S(2)}) copy-start(f32[2048,256]{1,0:T(8,128)} %copy-done.19) | copy-start | bytes 6291460
  66.5 1.0 copy-start.4
  67.4 1.4 %copy-start.21 = (f32[2048,256]{1,0:T(8,128)}, f32[2048,256]{1,0:T(8,128)S(1)}, u32[]{:S(2)}) copy-start(f32[2048,256]{1,0:T(8,128)S(1)} %get-tuple-element.30.total_in) | copy-start | bytes 6291460
  68.8 0.8 copy-start.8
  68.8 7.3 %copy-start.5 = (f32[2048,128]{1,0:T(8,128)S(1)}, f32[2048,128]{1,0:T(8,128)}, u32[]{:S(2)}) copy-start(f32[2048,128]{1,0:T(8,128)} %copy-done.4) | copy-start | bytes 3145732
  69.6 17.9 %collective-permute-start.7 = (bf16[1024,256]{1,0:T(8,128)(2,1)}, bf16[1024,256]{1,0:T(8,128)(2,1)S(1)}, u32[]{:S(2)}, u32[]{:S(2)}) collective-permute-start(bf16[1024,256]{1,0:T(8,128)(2,1)} %after.6.unit_ref), channel_id=1, source_target_pairs={{0,8},{8,0},{16,24},{24,16},{32,40},{40,32},{48,56},{56,48},{64,72... | collective-permute-start | bytes 1572872 | tf_op jit(solution)/shard_map/ppermute | solution.py:206
  74.2 10.2 %collective-permute-start.5 = (bf16[512,256]{1,0:T(8,128)(2,1)S(1)}, bf16[512,256]{1,0:T(8,128)(2,1)S(1)}, u32[]{:S(2)}, u32[]{:S(2)}) collective-permute-start(bf16[512,256]{1,0:T(8,128)(2,1)S(1)} %constant_dynamic-slice_fusion), channel_id=1, source_target_pairs={{0,16},{8,120},{16,32},{24,8},{32,48},{40,24},{48,64},{56,40},{64,... | collective-permute-start | bytes 786440 | tf_op jit(solution)/shard_map/ppermute | solution.py:205
  76.1 1.0 copy-start.9
  77.2 1.6 %copy-start.22 = (f32[2048,256]{1,0:T(8,128)S(1)}, f32[2048,256]{1,0:T(8,128)}, u32[]{:S(2)}) copy-start(f32[2048,256]{1,0:T(8,128)} %copy-done.21) | copy-start | bytes 6291460
  82.0 1.0 copy-start.6
  83.0 1.4 %copy-start.23 = (f32[2048,256]{1,0:T(8,128)}, f32[2048,256]{1,0:T(8,128)S(1)}, u32[]{:S(2)}) copy-start(f32[2048,256]{1,0:T(8,128)S(1)} %get-tuple-element.32.total_in) | copy-start | bytes 6291460
  84.4 0.7 copy-start.14
  85.1 9.9 %collective-permute-start.6 = (bf16[512,256]{1,0:T(8,128)(2,1)}, bf16[512,256]{1,0:T(8,128)(2,1)S(1)}, u32[]{:S(2)}, u32[]{:S(2)}) collective-permute-start(bf16[512,256]{1,0:T(8,128)(2,1)} %after.7.near_ref), channel_id=1, source_target_pairs={{0,8},{8,0},{16,24},{24,16},{32,40},{40,32},{48,56},{56,48},{64,72... | collective-permute-start | bytes 786440 | tf_op jit(solution)/shard_map/ppermute | solution.py:216
  87.5 1.2 copy-start.7
  88.8 1.6 %copy-start.24 = (f32[2048,256]{1,0:T(8,128)S(1)}, f32[2048,256]{1,0:T(8,128)}, u32[]{:S(2)}) copy-start(f32[2048,256]{1,0:T(8,128)} %copy-done.23) | copy-start | bytes 6291460
  90.3 4.6 %copy-start.15 = (bf16[512,256]{1,0:T(8,128)(2,1)S(1)}, bf16[512,256]{1,0:T(8,128)(2,1)}, u32[]{:S(2)}) copy-start(bf16[512,256]{1,0:T(8,128)(2,1)} %after.7.near_ref) | copy-start | bytes 786436
  93.6 1.4 %copy-start.25 = (f32[2048,256]{1,0:T(8,128)}, f32[2048,256]{1,0:T(8,128)S(1)}, u32[]{:S(2)}) copy-start(f32[2048,256]{1,0:T(8,128)S(1)} %get-tuple-element.33.total_in) | copy-start | bytes 6291460
  95.0 1.6 %copy-start.26 = (f32[2048,256]{1,0:T(8,128)S(1)}, f32[2048,256]{1,0:T(8,128)}, u32[]{:S(2)}) copy-start(f32[2048,256]{1,0:T(8,128)} %copy-done.25) | copy-start | bytes 6291460

commit v2 on v1

--- a/solution.py
+++ b/solution.py
@@ -97,11 +97,11 @@
 
 
 def last_kernel(scaled, near_ref, far_ref, bias_ref, total_in, largest_in, out_ref, total, largest):
+    del total_in, largest_in
+
     def masked(scores, half):
         return scores + bias_ref[half : half + 1, :]
 
-    total[...] = total_in[...]
-    largest[...] = largest_in[...]
     unit = jnp.concatenate([near_ref[...], far_ref[...]], axis=0)
     absorb(scaled, unit, masked, total, largest)
     heads = out_ref.shape[1] // HEAD_SIZE
@@ -117,23 +117,28 @@
 
 SMEM = pl.BlockSpec(memory_space=pltpu.SMEM)
 VMEM = pl.BlockSpec(memory_space=pltpu.VMEM)
-PARAMS = pltpu.CompilerParams(vmem_limit_bytes=40 * 2**20)
-
-
-def after_kernel(value_ref, other_ref, out_ref):
-    del value_ref, other_ref, out_ref
-
-
-def after(value, other):
+PARAMS = pltpu.CompilerParams(vmem_limit_bytes=16 * 2**20)
+
+
+def after_kernel(*refs):
+    del refs
+
+
+def after(value, *others):
     anywhere = pl.BlockSpec(memory_space=pl.ANY)
     return pl.pallas_call(
         after_kernel,
         out_shape=jax.ShapeDtypeStruct(value.shape, value.dtype),
-        in_specs=[anywhere] * 2,
+        in_specs=[anywhere] * (1 + len(others)),
         out_specs=anywhere,
         input_output_aliases={0: 0},
+        compiler_params=pltpu.CompilerParams(vmem_limit_bytes=2**20),
         name="after",
-    )(value, other)
+    )(value, *[held(other) for other in others])
+
+
+def held(value):
+    return pltpu.with_memory_space_constraint(value, pltpu.VMEM)
 
 
 def kernel_cost(rows, keys):
@@ -171,12 +176,12 @@
         return jax.ShapeDtypeStruct((rows, columns), dtype)
 
     state = [
-        shape(row_count, 2 * HEAD_SIZE, jnp.float32),
-        shape(row_count, HEAD_SIZE, jnp.float32),
+        pltpu.VMEM((row_count, 2 * HEAD_SIZE), jnp.float32),
+        pltpu.VMEM((row_count, HEAD_SIZE), jnp.float32),
     ]
     scaled, total, largest = pl.pallas_call(
         first_kernel,
-        out_shape=[shape(row_count, 2 * HEAD_SIZE, jnp.bfloat16)] + state,
+        out_shape=[pltpu.VMEM((row_count, 2 * HEAD_SIZE), jnp.bfloat16)] + state,
         in_specs=[SMEM] + [VMEM] * 3,
         out_specs=[VMEM] * 3,
         compiler_params=PARAMS,
@@ -194,7 +199,7 @@
             compiler_params=PARAMS,
             cost_estimate=kernel_cost(row_count, unit_rows),
             name="attend_next",
-        )(scaled, unit, bias, total, largest)
+        )(held(scaled), unit, bias, held(total), held(largest))
 
     unit = lax.ppermute(own_unit, "seq", ALONG_Z)
     for step in range(1, CHIPS_Z // 2):
@@ -208,27 +213,23 @@
         total, largest = attend_next(
             here, jnp.where(core == 0, lower, upper), total, largest
         )
-        halfway = largest
         total, largest = attend_next(
             other, jnp.where(core == 0, upper, lower), total, largest
         )
-    unit = after(unit, halfway)
+    unit = after(unit, largest)
     other = lax.ppermute(unit, "seq", OTHER_CORE)
     opposite = bias[CHIPS_Z // 2]
     opposite = jnp.where(core == 0, opposite, jnp.roll(opposite, unit_rows // 2, axis=1))
-    attended = pl.pallas_call(
+    attended, _, _ = pl.pallas_call(
         last_kernel,
-        out_shape=shape(queries.shape[0], queries.shape[1], jnp.bfloat16),
+        out_shape=[shape(queries.shape[0], queries.shape[1], jnp.bfloat16)] + state,
         in_specs=[VMEM] * 6,
-        out_specs=VMEM,
-        scratch_shapes=[
-            pltpu.VMEM((row_count, 2 * HEAD_SIZE), jnp.float32),
-            pltpu.VMEM((row_count, HEAD_SIZE), jnp.float32),
-        ],
+        out_specs=[VMEM] * 3,
+        input_output_aliases={4: 1, 5: 2},
         compiler_params=PARAMS,
         cost_estimate=kernel_cost(row_count, unit_rows),
         name="attend_last",
-    )(scaled, unit, other, opposite, total, largest)
+    )(held(scaled), unit, other, opposite, held(total), held(largest))
     return lax.all_to_all(attended, "tp", split_axis=0, concat_axis=1, tiled=True)
 
 

time: 131 us -> 114 us (0.87)
  local copies, waits for them, and re-layouts: 31.3 us -> 9.59 us
  waiting for transfers between devices: 1.48 us -> 7.61 us
  starting transfers between devices: 21.7 us -> 20.3 us
    unnamed x55 -> x17, local copies, waits for them, and re-layouts: 27.9 us -> 7.19 us
    ppermute x3, waiting for transfers between devices: 0.01 us -> 3.91 us  [on_device(): unit = lax.ppermute(unit, 'seq', ALONG_Z)]
    ppermute x3, starting transfers between devices: 10 us -> 8.41 us  [on_device(): other = lax.ppermute(here, 'seq', OTHER_CORE)]
  transfers between devices with their start and end apart: 8 -> 8, of which waited for: 1 -> 4; matrix products, arithmetic and copies ran while one was open for 3% -> 2% of each run, Pallas kernels for 18% -> 21%
where the time goes in v2:
time: 114 us; the launch traced here: 113 us
  blocking collectives  47.6 us (42%)
  Pallas kernels  26.7 us (23%)
  starting transfers between devices  20.3 us (18%)
  local copies, waits for them, and re-layouts  9.59 us (8%)
  waiting for transfers between devices  7.61 us (7%)
    all_to_all x1, blocking collectives, on_device(): lax.all_to_all(attended, 'tp', split_axis=0, concat_axis=1, tiled=True)  29.1 us
    pallas_call x6, Pallas kernels, attend_next(): pl.pallas_call(next_kernel, out_shape=state, in_specs=[VMEM] * 5, out_spe...  19.5 us
    all_gather x1, blocking collectives, on_device(): lax.all_gather(kv, 'seq', axis=0, tiled=True, axis_index_groups=COLUMNS)  18.5 us
    ppermute x3, starting transfers between devices, on_device(): other = lax.ppermute(here, 'seq', OTHER_CORE)  8.41 us
    unnamed x17, local copies, waits for them, and re-layouts  7.19 us
    ppermute x3, starting transfers between devices, on_device(): unit = lax.ppermute(unit, 'seq', ALONG_Z)  6.9 us
    ppermute x3, waiting for transfers between devices, on_device(): unit = lax.ppermute(unit, 'seq', ALONG_Z)  3.91 us
    pallas_call x1, Pallas kernels, on_device(): pl.pallas_call(first_kernel, out_shape=[pltpu.VMEM((row_count, 2 * HEAD_S...  3.85 us
  transfers between devices with their start and end apart: 8, of which 4 were waited for; matrix products, arithmetic and copies ran while one was open for 2% of the time, Pallas kernels for 21%

profile of v2, /device:TPU:16, one launch (start us, length us, event | category | flops | bytes accessed | tf_op | source)
XLA Modules:
  0.0 113.1 jit_solution(1401135773772811811)
XLA Ops:
  0.0 0.8 pad_maximum_fusion
  0.8 18.5 %all_gather.3.unit_ref = bf16[1024,256]{1,0:T(8,128)(2,1)S(1)} all-gather(bf16[128,256]{1,0:T(8,128)(2,1)S(1)} %pad_maximum_fusion), channel_id=1, replica_groups={{0,8,128,136,256,264,384,392},{16,24,144,152,272,280,400,408},{32,40,16..., dimensions={0}, use_global_device_ids=true | all-gather | bytes 589824 | tf_op jit(solution)/shard_map/all_gather | solution.py:159
  19.2 1.9 %collective-permute-start = (bf16[1024,256]{1,0:T(8,128)(2,1)S(1)}, bf16[1024,256]{1,0:T(8,128)(2,1)S(1)}, u32[]{:S(2)}, u32[]{:S(2)}) collective-permute-start(bf16[1024,256]{1,0:T(8,128)(2,1)S(1)} %all_gather.3.unit_ref), channel_id=1, source_target_pairs={{0,16},{8,120},{16,32},{24,8},{32,48},{40,24},{48,64},{56,40},{64,... | collective-permute-start | bytes 1572872 | tf_op jit(solution)/shard_map/ppermute | solution.py:204
  21.2 0.8 copy.27
  22.0 0.9 dynamic-slice_reduce_fusion.own_ref
  22.8 0.1 reshape.57
  22.9 0.1 copy.28
  23.0 0.1 dynamic-slice_add_fusion
  23.1 0.1 copy.29
  23.1 0.1 slice_reduce_fusion
  23.3 0.1 broadcast_in_dim.16
  23.3 0.1 broadcast_in_dim.17
  23.4 0.1 broadcast_in_dim.18
  23.5 0.1 lt.39
  23.6 0.0 copy-start
  23.6 1.0 copy-done
  24.6 3.8 %attend_first.1 = (bf16[2048,256]{1,0:T(8,128)(2,1)S(1)}, f32[2048,256]{1,0:T(8,128)S(1)}, f32[2048,128]{1,0:T(8,128)S(1)}) custom-call(s32[2]{0:T(128)S(1)} %dynamic-slice_reduce_fusion.own_ref, bf16[128,2048]{1,0:T(8,128)(2,1)S(1)} %copy-done, bf16[1024,256]{1,0:T(8,128)(2,1)S(1)} %all_gather.3.unit_ref, s32[1,1024]{1,0:T(1,128)S(1)} %and_add_fusion.pos_ref), custom_call_target="tpu_custom_call" | custom-call | flops 2147483648 | bytes 2097152 | tf_op jit(solution)/shard_map/attend_first/pallas_call | solution.py:182
  28.5 0.0 copy-start.5
  28.5 1.0 copy-done.5
  29.5 0.0 copy-start.1
  29.5 2.6 %collective-permute-done.refs_0_ = bf16[1024,256]{1,0:T(8,128)(2,1)S(1)} collective-permute-done((bf16[1024,256]{1,0:T(8,128)(2,1)S(1)}, bf16[1024,256]{1,0:T(8,128)(2,1)S(1)}, u32[]{:S(2)}, u32[]{:S(2)}) %collective-permute-start) | collective-permute-done | bytes 524320 | tf_op jit(solution)/shard_map/ppermute | solution.py:204
  32.1 0.0 copy-done.1
  32.1 4.5 %collective-permute-start.2 = (bf16[1024,256]{1,0:T(8,128)(2,1)S(1)}, bf16[1024,256]{1,0:T(8,128)(2,1)S(1)}, u32[]{:S(2)}, u32[]{:S(2)}) collective-permute-start(bf16[1024,256]{1,0:T(8,128)(2,1)S(1)} %after.4.unit_ref), channel_id=1, source_target_pairs={{0,8},{8,0},{16,24},{24,16},{32,40},{40,32},{48,56},{56,48},{64,72... | collective-permute-start | bytes 1572872 | tf_op jit(solution)/shard_map/ppermute | solution.py:211
  36.6 0.1 compare_select_fusion
  36.7 1.9 %collective-permute-start.1 = (bf16[1024,256]{1,0:T(8,128)(2,1)S(1)}, bf16[1024,256]{1,0:T(8,128)(2,1)S(1)}, u32[]{:S(2)}, u32[]{:S(2)}) collective-permute-start(bf16[1024,256]{1,0:T(8,128)(2,1)S(1)} %after.4.unit_ref), channel_id=1, source_target_pairs={{0,16},{8,120},{16,32},{24,8},{32,48},{40,24},{48,64},{56,40},{64,... | collective-permute-start | bytes 1572872 | tf_op jit(solution)/shard_map/ppermute | solution.py:210
  38.6 0.0 copy-start.2
  38.6 1.6 %copy-done.2 = f32[2048,256]{1,0:T(8,128)S(1)} copy-done((f32[2048,256]{1,0:T(8,128)S(1)}, f32[2048,256]{1,0:T(8,128)}, u32[]{:S(2)}) %copy-start.2) | copy-done | bytes 2097176
  40.2 0.0 copy-start.6
  40.2 1.2 %copy-done.6 = bf16[2048,256]{1,0:T(8,128)(2,1)S(1)} copy-done((bf16[2048,256]{1,0:T(8,128)(2,1)S(1)}, bf16[2048,256]{1,0:T(8,128)(2,1)}, u32[]{:S(2)}) %copy-start.6) | copy-done | bytes 1048600
  41.4 3.2 %attend_next.6 = (f32[2048,256]{1,0:T(8,128)S(1)}, f32[2048,128]{1,0:T(8,128)S(1)}) custom-call(bf16[2048,256]{1,0:T(8,128)(2,1)S(1)} %copy-done.6, bf16[1024,256]{1,0:T(8,128)(2,1)S(1)} %after.4.unit_ref, f32[2,1024]{1,0:T(2,128)S(1)} %get-tuple-element.43.bias_ref, f32[2048,256]{1,0:T(8,128)S(1)} %copy-done.2, ...), custom_call_target="tpu_custom_call", output_to_operand_aliasing={{0}: (3, {}), {1}: (4, {})} | custom-call | flops 2147483648 | bytes 2097152 | tf_op jit(solution)/shard_map/attend_next/pallas_call | solution.py:193
  44.7 0.0 collective-permute-done.2.unit_ref
  44.7 3.2 %attend_next.7 = (f32[2048,256]{1,0:T(8,128)S(1)}, f32[2048,128]{1,0:T(8,128)S(1)}) custom-call(bf16[2048,256]{1,0:T(8,128)(2,1)S(1)} %copy-done.6, bf16[1024,256]{1,0:T(8,128)(2,1)S(1)} %collective-permute-done.2.unit_ref, f32[2,1024]{1,0:T(2,128)S(1)} %get-tuple-element.42.bias_ref, ...), custom_call_target="tpu_custom_call", output_to_operand_aliasing={{0}: (3, {}), {1}: (4, {})} | custom-call | flops 2147483648 | bytes 2097152 | tf_op jit(solution)/shard_map/attend_next/pallas_call | solution.py:193
  47.9 1.0 collective-permute-done.1.refs_0_
  48.9 1.9 %collective-permute-start.4 = (bf16[1024,256]{1,0:T(8,128)(2,1)S(1)}, bf16[1024,256]{1,0:T(8,128)(2,1)S(1)}, u32[]{:S(2)}, u32[]{:S(2)}) collective-permute-start(bf16[1024,256]{1,0:T(8,128)(2,1)S(1)} %after.5.unit_ref), channel_id=1, source_target_pairs={{0,8},{8,0},{16,24},{24,16},{32,40},{40,32},{48,56},{56,48},{64,72... | collective-permute-start | bytes 1572872 | tf_op jit(solution)/shard_map/ppermute | solution.py:211
  50.9 2.8 %collective-permute-start.3 = (bf16[1024,256]{1,0:T(8,128)(2,1)S(1)}, bf16[1024,256]{1,0:T(8,128)(2,1)S(1)}, u32[]{:S(2)}, u32[]{:S(2)}) collective-permute-start(bf16[1024,256]{1,0:T(8,128)(2,1)S(1)} %after.5.unit_ref), channel_id=1, source_target_pairs={{0,16},{8,120},{16,32},{24,8},{32,48},{40,24},{48,64},{56,40},{64,... | collective-permute-start | bytes 1572872 | tf_op jit(solution)/shard_map/ppermute | solution.py:210
  53.7 3.3 %attend_next.8 = (f32[2048,256]{1,0:T(8,128)S(1)}, f32[2048,128]{1,0:T(8,128)S(1)}) custom-call(bf16[2048,256]{1,0:T(8,128)(2,1)S(1)} %copy-done.6, bf16[1024,256]{1,0:T(8,128)(2,1)S(1)} %after.5.unit_ref, f32[2,1024]{1,0:T(2,128)S(1)} %get-tuple-element.41.bias_ref, ...), custom_call_target="tpu_custom_call", output_to_operand_aliasing={{0}: (3, {}), {1}: (4, {})} | custom-call | flops 2147483648 | bytes 2097152 | tf_op jit(solution)/shard_map/attend_next/pallas_call | solution.py:193
  57.0 0.0 collective-permute-done.4.unit_ref
  57.0 3.2 %attend_next.9 = (f32[2048,256]{1,0:T(8,128)S(1)}, f32[2048,128]{1,0:T(8,128)S(1)}) custom-call(bf16[2048,256]{1,0:T(8,128)(2,1)S(1)} %copy-done.6, bf16[1024,256]{1,0:T(8,128)(2,1)S(1)} %collective-permute-done.4.unit_ref, f32[2,1024]{1,0:T(2,128)S(1)} %get-tuple-element.40.bias_ref, ...), custom_call_target="tpu_custom_call", output_to_operand_aliasing={{0}: (3, {}), {1}: (4, {})} | custom-call | flops 2147483648 | bytes 2097152 | tf_op jit(solution)/shard_map/attend_next/pallas_call | solution.py:193
  60.2 0.0 copy-start.3
  60.2 0.0 copy-start.7
  60.3 2.9 %collective-permute-done.3.refs_0_ = bf16[1024,256]{1,0:T(8,128)(2,1)S(1)} collective-permute-done((bf16[1024,256]{1,0:T(8,128)(2,1)S(1)}, bf16[1024,256]{1,0:T(8,128)(2,1)S(1)}, u32[]{:S(2)}, u32[]{:S(2)}) %collective-permute-start.3) | collective-permute-done | bytes 524320 | tf_op jit(solution)/shard_map/ppermute | solution.py:210
  63.2 0.0 copy-done.3
  63.2 2.0 %collective-permute-start.6 = (bf16[1024,256]{1,0:T(8,128)(2,1)S(1)}, bf16[1024,256]{1,0:T(8,128)(2,1)S(1)}, u32[]{:S(2)}, u32[]{:S(2)}) collective-permute-start(bf16[1024,256]{1,0:T(8,128)(2,1)S(1)} %after.6.unit_ref), channel_id=1, source_target_pairs={{0,8},{8,0},{16,24},{24,16},{32,40},{40,32},{48,56},{56,48},{64,72... | collective-permute-start | bytes 1572872 | tf_op jit(solution)/shard_map/ppermute | solution.py:211
  65.2 2.1 %collective-permute-start.5 = (bf16[512,256]{1,0:T(8,128)(2,1)S(1)}, bf16[512,256]{1,0:T(8,128)(2,1)S(1)}, u32[]{:S(2)}, u32[]{:S(2)}) collective-permute-start(bf16[512,256]{1,0:T(8,128)(2,1)S(1)} %constant_dynamic-slice_fusion), channel_id=1, source_target_pairs={{0,16},{8,120},{16,32},{24,8},{32,48},{40,24},{48,64},{56,40},{64,... | collective-permute-start | bytes 786440 | tf_op jit(solution)/shard_map/ppermute | solution.py:210
  67.4 0.0 copy-done.7
  67.4 0.0 copy-start.4
  67.4 1.6 %copy-done.4 = f32[2048,256]{1,0:T(8,128)S(1)} copy-done((f32[2048,256]{1,0:T(8,128)S(1)}, f32[2048,256]{1,0:T(8,128)}, u32[]{:S(2)}) %copy-start.4) | copy-done | bytes 2097176
  69.0 3.3 %attend_next.10 = (f32[2048,256]{1,0:T(8,128)S(1)}, f32[2048,128]{1,0:T(8,128)S(1)}) custom-call(bf16[2048,256]{1,0:T(8,128)(2,1)S(1)} %copy-done.7, bf16[1024,256]{1,0:T(8,128)(2,1)S(1)} %after.6.unit_ref, f32[2,1024]{1,0:T(2,128)S(1)} %get-tuple-element.39.bias_ref, f32[2048,256]{1,0:T(8,128)S(1)} %copy-done.4, ...), custom_call_target="tpu_custom_call", output_to_operand_aliasing={{0}: (3, {}), {1}: (4, {})} | custom-call | flops 2147483648 | bytes 2097152 | tf_op jit(solution)/shard_map/attend_next/pallas_call | solution.py:193
  72.2 0.0 collective-permute-done.6.unit_ref
  72.3 3.2 %attend_next.11 = (f32[2048,256]{1,0:T(8,128)S(1)}, f32[2048,128]{1,0:T(8,128)S(1)}) custom-call(bf16[2048,256]{1,0:T(8,128)(2,1)S(1)} %copy-done.7, bf16[1024,256]{1,0:T(8,128)(2,1)S(1)} %collective-permute-done.6.unit_ref, f32[2,1024]{1,0:T(2,128)S(1)} %get-tuple-element.38.bias_ref, ...), custom_call_target="tpu_custom_call", output_to_operand_aliasing={{0}: (3, {}), {1}: (4, {})} | custom-call | flops 2147483648 | bytes 2097152 | tf_op jit(solution)/shard_map/attend_next/pallas_call | solution.py:193
  75.5 0.0 collective-permute-done.5.refs_0_
  75.5 3.1 %collective-permute-start.7 = (bf16[512,256]{1,0:T(8,128)(2,1)S(1)}, bf16[512,256]{1,0:T(8,128)(2,1)S(1)}, u32[]{:S(2)}, u32[]{:S(2)}) collective-permute-start(bf16[512,256]{1,0:T(8,128)(2,1)S(1)} %after.7.near_ref), channel_id=1, source_target_pairs={{0,8},{8,0},{16,24},{24,16},{32,40},{40,32},{48,56},{56,48},{64,72... | collective-permute-start | bytes 786440 | tf_op jit(solution)/shard_map/ppermute | solution.py:220
  78.6 1.1 collective-permute-done.7.far_ref
  79.8 3.4 %attend_last.1 = (bf16[128,2048]{1,0:T(8,128)(2,1)S(1)}, f32[2048,256]{1,0:T(8,128)S(1)}, f32[2048,128]{1,0:T(8,128)S(1)}) custom-call(bf16[2048,256]{1,0:T(8,128)(2,1)S(1)} %copy-done.7, bf16[512,256]{1,0:T(8,128)(2,1)S(1)} %after.7.near_ref, bf16[512,256]{1,0:T(8,128)(2,1)S(1)} %collective-permute-done.7.far_ref, ...), custom_call_target="tpu_custom_call", output_to_operand_aliasing={{1}: (4, {}), {2}: (5, {})} | custom-call | flops 2147483648 | bytes 2097152 | tf_op jit(solution)/shard_map/attend_last/pallas_call | solution.py:223
  83.2 29.1 %all_to_all.19 = bf16[8,16,2048]{2,1,0:T(8,128)(2,1)S(1)} all-to-all(bf16[8,16,2048]{2,1,0:T(8,128)(2,1)S(1)} %bitcast.22), channel_id=1, replica_groups=mesh['seq'=64,'tp'=8] {'tp'}, dimensions={0} | all-to-all | bytes 1048576 | tf_op jit(solution)/shard_map/all_to_all | solution.py:233
  112.3 0.8 copy.31
  (9 shorter events, 0.1 us)
Async XLA Ops:
  19.2 12.8 %collective-permute-start = (bf16[1024,256]{1,0:T(8,128)(2,1)S(1)}, bf16[1024,256]{1,0:T(8,128)(2,1)S(1)}, u32[]{:S(2)}, u32[]{:S(2)}) collective-permute-start(bf16[1024,256]{1,0:T(8,128)(2,1)S(1)} %all_gather.3.unit_ref), channel_id=1, source_target_pairs={{0,16},{8,120},{16,32},{24,8},{32,48},{40,24},{48,64},{56,40},{64,... | collective-permute-start | bytes 1572872 | tf_op jit(solution)/shard_map/ppermute | solution.py:204
  23.6 1.0 copy-start
  28.5 1.0 copy-start.5
  29.5 2.6 %copy-start.1 = (f32[2048,256]{1,0:T(8,128)}, f32[2048,256]{1,0:T(8,128)S(1)}, u32[]{:S(2)}) copy-start(f32[2048,256]{1,0:T(8,128)S(1)} %get-tuple-element.23.total_in) | copy-start | bytes 6291460
  32.1 12.6 %collective-permute-start.2 = (bf16[1024,256]{1,0:T(8,128)(2,1)S(1)}, bf16[1024,256]{1,0:T(8,128)(2,1)S(1)}, u32[]{:S(2)}, u32[]{:S(2)}) collective-permute-start(bf16[1024,256]{1,0:T(8,128)(2,1)S(1)} %after.4.unit_ref), channel_id=1, source_target_pairs={{0,8},{8,0},{16,24},{24,16},{32,40},{40,32},{48,56},{56,48},{64,72... | collective-permute-start | bytes 1572872 | tf_op jit(solution)/shard_map/ppermute | solution.py:211
  36.7 12.3 %collective-permute-start.1 = (bf16[1024,256]{1,0:T(8,128)(2,1)S(1)}, bf16[1024,256]{1,0:T(8,128)(2,1)S(1)}, u32[]{:S(2)}, u32[]{:S(2)}) collective-permute-start(bf16[1024,256]{1,0:T(8,128)(2,1)S(1)} %after.4.unit_ref), channel_id=1, source_target_pairs={{0,16},{8,120},{16,32},{24,8},{32,48},{40,24},{48,64},{56,40},{64,... | collective-permute-start | bytes 1572872 | tf_op jit(solution)/shard_map/ppermute | solution.py:210
  38.6 1.6 %copy-start.2 = (f32[2048,256]{1,0:T(8,128)S(1)}, f32[2048,256]{1,0:T(8,128)}, u32[]{:S(2)}) copy-start(f32[2048,256]{1,0:T(8,128)} %copy-done.1) | copy-start | bytes 6291460
  40.2 1.2 %copy-start.6 = (bf16[2048,256]{1,0:T(8,128)(2,1)S(1)}, bf16[2048,256]{1,0:T(8,128)(2,1)}, u32[]{:S(2)}) copy-start(bf16[2048,256]{1,0:T(8,128)(2,1)} %copy-done.5) | copy-start | bytes 3145732
  48.9 8.0 %collective-permute-start.4 = (bf16[1024,256]{1,0:T(8,128)(2,1)S(1)}, bf16[1024,256]{1,0:T(8,128)(2,1)S(1)}, u32[]{:S(2)}, u32[]{:S(2)}) collective-permute-start(bf16[1024,256]{1,0:T(8,128)(2,1)S(1)} %after.5.unit_ref), channel_id=1, source_target_pairs={{0,8},{8,0},{16,24},{24,16},{32,40},{40,32},{48,56},{56,48},{64,72... | collective-permute-start | bytes 1572872 | tf_op jit(solution)/shard_map/ppermute | solution.py:211
  50.9 12.3 %collective-permute-start.3 = (bf16[1024,256]{1,0:T(8,128)(2,1)S(1)}, bf16[1024,256]{1,0:T(8,128)(2,1)S(1)}, u32[]{:S(2)}, u32[]{:S(2)}) collective-permute-start(bf16[1024,256]{1,0:T(8,128)(2,1)S(1)} %after.5.unit_ref), channel_id=1, source_target_pairs={{0,16},{8,120},{16,32},{24,8},{32,48},{40,24},{48,64},{56,40},{64,... | collective-permute-start | bytes 1572872 | tf_op jit(solution)/shard_map/ppermute | solution.py:210
  60.2 2.9 %copy-start.3 = (f32[2048,256]{1,0:T(8,128)}, f32[2048,256]{1,0:T(8,128)S(1)}, u32[]{:S(2)}) copy-start(f32[2048,256]{1,0:T(8,128)S(1)} %get-tuple-element.31.total_in) | copy-start | bytes 6291460
  60.2 7.1 %copy-start.7 = (bf16[2048,256]{1,0:T(8,128)(2,1)S(1)}, bf16[2048,256]{1,0:T(8,128)(2,1)}, u32[]{:S(2)}) copy-start(bf16[2048,256]{1,0:T(8,128)(2,1)} %copy-done.5) | copy-start | bytes 3145732
  63.2 9.1 %collective-permute-start.6 = (bf16[1024,256]{1,0:T(8,128)(2,1)S(1)}, bf16[1024,256]{1,0:T(8,128)(2,1)S(1)}, u32[]{:S(2)}, u32[]{:S(2)}) collective-permute-start(bf16[1024,256]{1,0:T(8,128)(2,1)S(1)} %after.6.unit_ref), channel_id=1, source_target_pairs={{0,8},{8,0},{16,24},{24,16},{32,40},{40,32},{48,56},{56,48},{64,72... | collective-permute-start | bytes 1572872 | tf_op jit(solution)/shard_map/ppermute | solution.py:211
  65.2 10.3 %collective-permute-start.5 = (bf16[512,256]{1,0:T(8,128)(2,1)S(1)}, bf16[512,256]{1,0:T(8,128)(2,1)S(1)}, u32[]{:S(2)}, u32[]{:S(2)}) collective-permute-start(bf16[512,256]{1,0:T(8,128)(2,1)S(1)} %constant_dynamic-slice_fusion), channel_id=1, source_target_pairs={{0,16},{8,120},{16,32},{24,8},{32,48},{40,24},{48,64},{56,40},{64,... | collective-permute-start | bytes 786440 | tf_op jit(solution)/shard_map/ppermute | solution.py:210
  67.4 1.6 %copy-start.4 = (f32[2048,256]{1,0:T(8,128)S(1)}, f32[2048,256]{1,0:T(8,128)}, u32[]{:S(2)}) copy-start(f32[2048,256]{1,0:T(8,128)} %copy-done.3) | copy-start | bytes 6291460
  75.5 4.2 %collective-permute-start.7 = (bf16[512,256]{1,0:T(8,128)(2,1)S(1)}, bf16[512,256]{1,0:T(8,128)(2,1)S(1)}, u32[]{:S(2)}, u32[]{:S(2)}) collective-permute-start(bf16[512,256]{1,0:T(8,128)(2,1)S(1)} %after.7.near_ref), channel_id=1, source_target_pairs={{0,8},{8,0},{16,24},{24,16},{32,40},{40,32},{48,56},{56,48},{64,72... | collective-permute-start | bytes 786440 | tf_op jit(solution)/shard_map/ppermute | solution.py:220

commit v3 on v2

--- a/solution.py
+++ b/solution.py
@@ -1,3 +1,4 @@
+import functools
 import math
 
 import jax
@@ -59,7 +60,8 @@
         largest[rows, :] = new
 
 
-def first_kernel(own_ref, query_ref, unit_ref, pos_ref, scaled, total, largest):
+def first_kernel(own_ref, query_ref, unit_ref, pos_ref, bias_ref, scaled, total, largest):
+    del bias_ref
     heads = query_ref.shape[1] // HEAD_SIZE
     scale = math.log2(math.e) / math.sqrt(HEAD_SIZE)
     for half in range(2):
@@ -87,23 +89,24 @@
     absorb(scaled, unit_ref[...], masked, total, largest)
 
 
-def next_kernel(scaled, unit_ref, bias_ref, total_in, largest_in, total, largest):
+def next_kernel(turn, scaled, unit_ref, bias_ref, total_in, largest_in, total, largest):
     del total_in, largest_in
 
     def masked(scores, half):
-        return scores + bias_ref[half : half + 1, :]
+        row = 2 * turn + half
+        return scores + bias_ref[row : row + 1, :]
 
     absorb(scaled, unit_ref[...], masked, total, largest)
 
 
-def last_kernel(scaled, near_ref, far_ref, bias_ref, total_in, largest_in, out_ref, total, largest):
+def last_kernel(turn, scaled, unit_ref, bias_ref, total_in, largest_in, out_ref, total, largest):
     del total_in, largest_in
 
     def masked(scores, half):
-        return scores + bias_ref[half : half + 1, :]
-
-    unit = jnp.concatenate([near_ref[...], far_ref[...]], axis=0)
-    absorb(scaled, unit, masked, total, largest)
+        row = 2 * turn + half
+        return scores + bias_ref[row : row + 1, :]
+
+    absorb(scaled, unit_ref[...], masked, total, largest)
     heads = out_ref.shape[1] // HEAD_SIZE
     for half in range(2):
         for head in range(heads):
@@ -168,9 +171,19 @@
     own_pos = positions[:1] + lax.rem(
         lax.broadcasted_iota(jnp.int32, (1, unit_rows), 1), HALF_ROWS
     )
+    distances = [
+        distance
+        for step in range(1, CHIPS_Z // 2)
+        for distance in (CHIPS_Z - step, step)
+    ] + [CHIPS_Z // 2]
+    forward = jnp.stack([positions[distance] for distance in distances])
+    backward = jnp.stack([positions[CHIPS_Z - distance] for distance in distances])
     bias = jnp.where(
-        positions[:, None, :] < own_starts[None, :, None], 0.0, MASKED_SCORE
+        jnp.where(core == 0, forward, backward)[:, None, :] < own_starts[None, :, None],
+        0.0,
+        MASKED_SCORE,
     ).astype(jnp.float32)
+    bias = bias.reshape(-1, unit_rows)
 
     def shape(rows, columns, dtype):
         return jax.ShapeDtypeStruct((rows, columns), dtype)
@@ -182,16 +195,16 @@
     scaled, total, largest = pl.pallas_call(
         first_kernel,
         out_shape=[pltpu.VMEM((row_count, 2 * HEAD_SIZE), jnp.bfloat16)] + state,
-        in_specs=[SMEM] + [VMEM] * 3,
+        in_specs=[SMEM] + [VMEM] * 3 + [pl.BlockSpec(memory_space=pl.ANY)],
         out_specs=[VMEM] * 3,
         compiler_params=PARAMS,
         cost_estimate=kernel_cost(row_count, unit_rows),
         name="attend_first",
-    )(own_starts, queries, own_unit, own_pos)
-
-    def attend_next(unit, bias, total, largest):
+    )(own_starts, queries, own_unit, own_pos, bias)
+
+    def attend_next(turn, unit, total, largest):
         return pl.pallas_call(
-            next_kernel,
+            functools.partial(next_kernel, turn),
             out_shape=state,
             in_specs=[VMEM] * 5,
             out_specs=[VMEM] * 2,
@@ -202,34 +215,28 @@
         )(held(scaled), unit, bias, held(total), held(largest))
 
     unit = lax.ppermute(own_unit, "seq", ALONG_Z)
-    for step in range(1, CHIPS_Z // 2):
-        unit = after(unit, largest)
-        here = unit
-        if step + 1 == CHIPS_Z // 2:
-            unit = lax.dynamic_slice_in_dim(unit, core * (unit_rows // 2), unit_rows // 2, 0)
-        unit = lax.ppermute(unit, "seq", ALONG_Z)
-        other = lax.ppermute(here, "seq", OTHER_CORE)
-        lower, upper = bias[CHIPS_Z - step], bias[step]
-        total, largest = attend_next(
-            here, jnp.where(core == 0, lower, upper), total, largest
-        )
-        total, largest = attend_next(
-            other, jnp.where(core == 0, upper, lower), total, largest
-        )
+    here = after(unit, largest)
+    unit = lax.ppermute(here, "seq", ALONG_Z)
+    total, largest = attend_next(0, here, total, largest)
+    other = lax.ppermute(after(here, largest), "seq", OTHER_CORE)
+    for step in range(2, CHIPS_Z // 2):
+        here = after(unit, largest)
+        unit = lax.ppermute(here, "seq", ALONG_Z)
+        total, largest = attend_next(2 * step - 3, other, total, largest)
+        other = lax.ppermute(after(here, largest), "seq", OTHER_CORE)
+        total, largest = attend_next(2 * step - 2, here, total, largest)
     unit = after(unit, largest)
-    other = lax.ppermute(unit, "seq", OTHER_CORE)
-    opposite = bias[CHIPS_Z // 2]
-    opposite = jnp.where(core == 0, opposite, jnp.roll(opposite, unit_rows // 2, axis=1))
+    total, largest = attend_next(len(distances) - 2, other, total, largest)
     attended, _, _ = pl.pallas_call(
-        last_kernel,
+        functools.partial(last_kernel, len(distances) - 1),
         out_shape=[shape(queries.shape[0], queries.shape[1], jnp.bfloat16)] + state,
-        in_specs=[VMEM] * 6,
+        in_specs=[VMEM] * 5,
         out_specs=[VMEM] * 3,
-        input_output_aliases={4: 1, 5: 2},
+        input_output_aliases={3: 1, 4: 2},
         compiler_params=PARAMS,
         cost_estimate=kernel_cost(row_count, unit_rows),
         name="attend_last",
-    )(held(scaled), unit, other, opposite, held(total), held(largest))
+    )(held(scaled), unit, bias, held(total), held(largest))
     return lax.all_to_all(attended, "tp", split_axis=0, concat_axis=1, tiled=True)
 
 

time: 114 us -> 108 us (0.947)
  local copies, waits for them, and re-layouts: 9.59 us -> 5.54 us
  starting transfers between devices: 20.3 us -> 16.5 us
  waiting for transfers between devices: 7.61 us -> 10.3 us
    unnamed x17 -> x5, local copies, waits for them, and re-layouts: 7.19 us -> 1.89 us
    ppermute x7 -> x6, starting transfers between devices: 18.4 us -> 14.6 us  [the longest x3 8.36 us: on_device(): other = lax.ppermute(after(here, largest), 'seq', OTHER_CORE)]
    ppermute x7 -> x6, waiting for transfers between devices: 5.03 us -> 7.86 us  [the longest x3 7.85 us: on_device(): unit = lax.ppermute(here, 'seq', ALONG_Z)]
  transfers between devices with their start and end apart: 8 -> 7, of which waited for: 4 -> 3; matrix products, arithmetic and copies ran while one was open for 2% -> 4% of each run, Pallas kernels for 21% -> 18%
where the time goes in v3:
time: 108 us; the launch traced here: 107 us
  blocking collectives  47.3 us (44%)
  Pallas kernels  26.4 us (24%)
  starting transfers between devices  16.5 us (15%)
  waiting for transfers between devices  10.3 us (10%)
  local copies, waits for them, and re-layouts  5.54 us (5%)
    all_to_all x1, blocking collectives, on_device(): lax.all_to_all(attended, 'tp', split_axis=0, concat_axis=1, tiled=True)  28.8 us
    pallas_call x6, Pallas kernels, attend_next(): pl.pallas_call(functools.partial(next_kernel, turn), out_shape=state, in_...  19.4 us
    all_gather x1, blocking collectives, on_device(): lax.all_gather(kv, 'seq', axis=0, tiled=True, axis_index_groups=COLUMNS)  18.5 us
    ppermute x3, starting transfers between devices, on_device(): other = lax.ppermute(after(here, largest), 'seq', OTHER_CORE)  8.36 us
    ppermute x3, waiting for transfers between devices, on_device(): unit = lax.ppermute(here, 'seq', ALONG_Z)  7.85 us
    ppermute x3, starting transfers between devices, on_device(): unit = lax.ppermute(here, 'seq', ALONG_Z)  6.25 us
    pallas_call x1, Pallas kernels, on_device(): pl.pallas_call(first_kernel, out_shape=[pltpu.VMEM((row_count, 2 * HEAD_S...  3.61 us
    pallas_call x1, Pallas kernels, on_device(): pl.pallas_call(functools.partial(last_kernel, len(distances) - 1), out_sh...  3.3 us
  transfers between devices with their start and end apart: 7, of which 3 were waited for; matrix products, arithmetic and copies ran while one was open for 4% of the time, Pallas kernels for 18%

profile of v3, /device:TPU:16, one launch (start us, length us, event | category | flops | bytes accessed | tf_op | source)
XLA Modules:
  0.0 107.2 jit_solution(407377233063315196)
XLA Ops:
  0.0 0.8 pad_maximum_fusion
  0.8 18.5 %all_gather.3.unit_ref = bf16[1024,256]{1,0:T(8,128)(2,1)S(1)} all-gather(bf16[128,256]{1,0:T(8,128)(2,1)S(1)} %pad_maximum_fusion), channel_id=1, replica_groups={{0,8,128,136,256,264,384,392},{16,24,144,152,272,280,400,408},{32,40,16..., dimensions={0}, use_global_device_ids=true | all-gather | bytes 589824 | tf_op jit(solution)/shard_map/all_gather | solution.py:162
  19.2 1.9 %collective-permute-start = (bf16[1024,256]{1,0:T(8,128)(2,1)S(1)}, bf16[1024,256]{1,0:T(8,128)(2,1)S(1)}, u32[]{:S(2)}, u32[]{:S(2)}) collective-permute-start(bf16[1024,256]{1,0:T(8,128)(2,1)S(1)} %all_gather.3.unit_ref), channel_id=1, source_target_pairs={{0,16},{8,120},{16,32},{24,8},{32,48},{40,24},{48,64},{56,40},{64,... | collective-permute-start | bytes 1572872 | tf_op jit(solution)/shard_map/ppermute | solution.py:217
  21.2 0.8 copy.29
  22.0 0.1 reshape.195
  22.0 0.1 copy.30
  22.1 0.1 dynamic-slice_add_fusion
  22.2 0.3 slice_reduce_fusion
  22.5 0.1 broadcast_in_dim.31
  22.6 0.1 stack.20
  22.7 0.1 broadcast_in_dim.32
  22.7 0.1 stack.21
  22.8 0.1 broadcast_in_dim.33
  22.9 0.1 stack.22
  23.0 0.1 broadcast_in_dim.34
  23.0 0.1 stack.23
  23.1 0.1 broadcast_in_dim.35
  23.2 0.1 stack.24
  23.3 0.1 broadcast_in_dim.36
  23.3 0.1 stack.25
  23.4 0.1 broadcast_in_dim.37
  23.5 0.1 stack.26
  23.6 0.1 stack.28
  23.6 0.1 stack.27
  23.7 0.1 broadcast_in_dim.29
  23.8 0.1 broadcast_in_dim.30
  24.0 0.9 dynamic-slice_reduce_fusion.own_ref
  24.8 0.1 lt.44
  24.9 0.1 compare_select_fusion.bias_ref
  25.0 0.0 copy-start
  25.0 1.0 copy-done
  26.0 3.6 %attend_first.1 = (bf16[2048,256]{1,0:T(8,128)(2,1)S(1)}, f32[2048,256]{1,0:T(8,128)S(1)}, f32[2048,128]{1,0:T(8,128)S(1)}) custom-call(s32[2]{0:T(128)S(1)} %dynamic-slice_reduce_fusion.own_ref, bf16[128,2048]{1,0:T(8,128)(2,1)S(1)} %copy-done, bf16[1024,256]{1,0:T(8,128)(2,1)S(1)} %all_gather.3.unit_ref, s32[1,1024]{1,0:T(1,128)S(1)} %and_add_fusion.pos_ref, ...), custom_call_target="tpu_custom_call" | custom-call | flops 2147483648 | bytes 2097152 | tf_op jit(solution)/shard_map/attend_first/pallas_call | solution.py:195
  29.7 2.4 %collective-permute-done.refs_0_ = bf16[1024,256]{1,0:T(8,128)(2,1)S(1)} collective-permute-done((bf16[1024,256]{1,0:T(8,128)(2,1)S(1)}, bf16[1024,256]{1,0:T(8,128)(2,1)S(1)}, u32[]{:S(2)}, u32[]{:S(2)}) %collective-permute-start) | collective-permute-done | bytes 524320 | tf_op jit(solution)/shard_map/ppermute | solution.py:217
  32.1 1.9 %collective-permute-start.1 = (bf16[1024,256]{1,0:T(8,128)(2,1)S(1)}, bf16[1024,256]{1,0:T(8,128)(2,1)S(1)}, u32[]{:S(2)}, u32[]{:S(2)}) collective-permute-start(bf16[1024,256]{1,0:T(8,128)(2,1)S(1)} %after.7.unit_ref.refs_0_), channel_id=1, source_target_pairs={{0,16},{8,120},{16,32},{24,8},{32,48},{40,24},{48,64},{56,40},{64,... | collective-permute-start | bytes 1572872 | tf_op jit(solution)/shard_map/ppermute | solution.py:219
  34.0 3.2 %attend_next.6 = (f32[2048,256]{1,0:T(8,128)S(1)}, f32[2048,128]{1,0:T(8,128)S(1)}) custom-call(bf16[2048,256]{1,0:T(8,128)(2,1)S(1)} %get-tuple-element.21.scaled, bf16[1024,256]{1,0:T(8,128)(2,1)S(1)} %after.7.unit_ref.refs_0_, f32[14,1024]{1,0:T(8,128)S(1)} %compare_select_fusion.bias_ref, ...), custom_call_target="tpu_custom_call", output_to_operand_aliasing={{0}: (3, {}), {1}: (4, {})} | custom-call | flops 2147483648 | bytes 2097152 | tf_op jit(solution)/shard_map/attend_next/pallas_call | solution.py:206
  37.2 7.1 %collective-permute-done.1.refs_0_ = bf16[1024,256]{1,0:T(8,128)(2,1)S(1)} collective-permute-done((bf16[1024,256]{1,0:T(8,128)(2,1)S(1)}, bf16[1024,256]{1,0:T(8,128)(2,1)S(1)}, u32[]{:S(2)}, u32[]{:S(2)}) %collective-permute-start.1) | collective-permute-done | bytes 524320 | tf_op jit(solution)/shard_map/ppermute | solution.py:219
  44.3 1.9 %collective-permute-start.3 = (bf16[1024,256]{1,0:T(8,128)(2,1)S(1)}, bf16[1024,256]{1,0:T(8,128)(2,1)S(1)}, u32[]{:S(2)}, u32[]{:S(2)}) collective-permute-start(bf16[1024,256]{1,0:T(8,128)(2,1)S(1)} %after.9), channel_id=1, source_target_pairs={{0,8},{8,0},{16,24},{24,16},{32,40},{40,32},{48,56},{56,48},{64,72... | collective-permute-start | bytes 1572872 | tf_op jit(solution)/shard_map/ppermute | solution.py:221
  46.3 1.9 %collective-permute-start.2 = (bf16[1024,256]{1,0:T(8,128)(2,1)S(1)}, bf16[1024,256]{1,0:T(8,128)(2,1)S(1)}, u32[]{:S(2)}, u32[]{:S(2)}) collective-permute-start(bf16[1024,256]{1,0:T(8,128)(2,1)S(1)} %after.8.unit_ref), channel_id=1, source_target_pairs={{0,16},{8,120},{16,32},{24,8},{32,48},{40,24},{48,64},{56,40},{64,... | collective-permute-start | bytes 1572872 | tf_op jit(solution)/shard_map/ppermute | solution.py:224
  48.2 0.0 collective-permute-done.3.unit_ref
  48.3 3.2 %attend_next.7 = (f32[2048,256]{1,0:T(8,128)S(1)}, f32[2048,128]{1,0:T(8,128)S(1)}) custom-call(bf16[2048,256]{1,0:T(8,128)(2,1)S(1)} %get-tuple-element.21.scaled, bf16[1024,256]{1,0:T(8,128)(2,1)S(1)} %collective-permute-done.3.unit_ref, f32[14,1024]{1,0:T(8,128)S(1)} %compare_select_fusion.bias_ref, ...), custom_call_target="tpu_custom_call", output_to_operand_aliasing={{0}: (3, {}), {1}: (4, {})} | custom-call | flops 2147483648 | bytes 2097152 | tf_op jit(solution)/shard_map/attend_next/pallas_call | solution.py:206
  51.5 3.1 %collective-permute-start.5 = (bf16[1024,256]{1,0:T(8,128)(2,1)S(1)}, bf16[1024,256]{1,0:T(8,128)(2,1)S(1)}, u32[]{:S(2)}, u32[]{:S(2)}) collective-permute-start(bf16[1024,256]{1,0:T(8,128)(2,1)S(1)} %after.11), channel_id=1, source_target_pairs={{0,8},{8,0},{16,24},{24,16},{32,40},{40,32},{48,56},{56,48},{64,72... | collective-permute-start | bytes 1572872 | tf_op jit(solution)/shard_map/ppermute | solution.py:226
  54.6 3.2 %attend_next.8 = (f32[2048,256]{1,0:T(8,128)S(1)}, f32[2048,128]{1,0:T(8,128)S(1)}) custom-call(bf16[2048,256]{1,0:T(8,128)(2,1)S(1)} %get-tuple-element.21.scaled, bf16[1024,256]{1,0:T(8,128)(2,1)S(1)} %after.8.unit_ref, f32[14,1024]{1,0:T(8,128)S(1)} %compare_select_fusion.bias_ref, ...), custom_call_target="tpu_custom_call", output_to_operand_aliasing={{0}: (3, {}), {1}: (4, {})} | custom-call | flops 2147483648 | bytes 2097152 | tf_op jit(solution)/shard_map/attend_next/pallas_call | solution.py:206
  57.9 0.7 collective-permute-done.2.refs_0_
  58.6 2.4 %collective-permute-start.4 = (bf16[1024,256]{1,0:T(8,128)(2,1)S(1)}, bf16[1024,256]{1,0:T(8,128)(2,1)S(1)}, u32[]{:S(2)}, u32[]{:S(2)}) collective-permute-start(bf16[1024,256]{1,0:T(8,128)(2,1)S(1)} %after.10.unit_ref), channel_id=1, source_target_pairs={{0,16},{8,120},{16,32},{24,8},{32,48},{40,24},{48,64},{56,40},{64,... | collective-permute-start | bytes 1572872 | tf_op jit(solution)/shard_map/ppermute | solution.py:224
  61.1 0.0 collective-permute-done.5.unit_ref
  61.1 3.2 %attend_next.9 = (f32[2048,256]{1,0:T(8,128)S(1)}, f32[2048,128]{1,0:T(8,128)S(1)}) custom-call(bf16[2048,256]{1,0:T(8,128)(2,1)S(1)} %get-tuple-element.21.scaled, bf16[1024,256]{1,0:T(8,128)(2,1)S(1)} %collective-permute-done.5.unit_ref, f32[14,1024]{1,0:T(8,128)S(1)} %compare_select_fusion.bias_ref, ...), custom_call_target="tpu_custom_call", output_to_operand_aliasing={{0}: (3, {}), {1}: (4, {})} | custom-call | flops 2147483648 | bytes 2097152 | tf_op jit(solution)/shard_map/attend_next/pallas_call | solution.py:206
  64.3 3.4 %collective-permute-start.6 = (bf16[1024,256]{1,0:T(8,128)(2,1)S(1)}, bf16[1024,256]{1,0:T(8,128)(2,1)S(1)}, u32[]{:S(2)}, u32[]{:S(2)}) collective-permute-start(bf16[1024,256]{1,0:T(8,128)(2,1)S(1)} %after.13), channel_id=1, source_target_pairs={{0,8},{8,0},{16,24},{24,16},{32,40},{40,32},{48,56},{56,48},{64,72... | collective-permute-start | bytes 1572872 | tf_op jit(solution)/shard_map/ppermute | solution.py:226
  67.7 3.2 %attend_next.10 = (f32[2048,256]{1,0:T(8,128)S(1)}, f32[2048,128]{1,0:T(8,128)S(1)}) custom-call(bf16[2048,256]{1,0:T(8,128)(2,1)S(1)} %get-tuple-element.21.scaled, bf16[1024,256]{1,0:T(8,128)(2,1)S(1)} %after.10.unit_ref, f32[14,1024]{1,0:T(8,128)S(1)} %compare_select_fusion.bias_ref, ...), custom_call_target="tpu_custom_call", output_to_operand_aliasing={{0}: (3, {}), {1}: (4, {})} | custom-call | flops 2147483648 | bytes 2097152 | tf_op jit(solution)/shard_map/attend_next/pallas_call | solution.py:206
  70.9 0.0 collective-permute-done.4.refs_0_
  71.0 0.0 collective-permute-done.6.unit_ref
  71.0 3.2 %attend_next.11 = (f32[2048,256]{1,0:T(8,128)S(1)}, f32[2048,128]{1,0:T(8,128)S(1)}) custom-call(bf16[2048,256]{1,0:T(8,128)(2,1)S(1)} %get-tuple-element.21.scaled, bf16[1024,256]{1,0:T(8,128)(2,1)S(1)} %collective-permute-done.6.unit_ref, f32[14,1024]{1,0:T(8,128)S(1)} %compare_select_fusion.bias_ref, ...), custom_call_target="tpu_custom_call", output_to_operand_aliasing={{0}: (3, {}), {1}: (4, {})} | custom-call | flops 2147483648 | bytes 2097152 | tf_op jit(solution)/shard_map/attend_next/pallas_call | solution.py:206
  74.2 3.3 %attend_last.1 = (bf16[128,2048]{1,0:T(8,128)(2,1)S(1)}, f32[2048,256]{1,0:T(8,128)S(1)}, f32[2048,128]{1,0:T(8,128)S(1)}) custom-call(bf16[2048,256]{1,0:T(8,128)(2,1)S(1)} %get-tuple-element.21.scaled, bf16[1024,256]{1,0:T(8,128)(2,1)S(1)} %after.12.unit_ref, ...), custom_call_target="tpu_custom_call", output_to_operand_aliasing={{1}: (3, {}), {2}: (4, {})} | custom-call | flops 2147483648 | bytes 2097152 | tf_op jit(solution)/shard_map/attend_last/pallas_call | solution.py:230
  77.5 28.8 %all_to_all.19 = bf16[8,16,2048]{2,1,0:T(8,128)(2,1)S(1)} all-to-all(bf16[8,16,2048]{2,1,0:T(8,128)(2,1)S(1)} %bitcast.6), channel_id=1, replica_groups=mesh['seq'=64,'tp'=8] {'tp'}, dimensions={0} | all-to-all | bytes 1048576 | tf_op jit(solution)/shard_map/all_to_all | solution.py:240
  106.3 0.8 copy.32
  (14 shorter events, 0.2 us)
Async XLA Ops:
  19.2 12.8 %collective-permute-start = (bf16[1024,256]{1,0:T(8,128)(2,1)S(1)}, bf16[1024,256]{1,0:T(8,128)(2,1)S(1)}, u32[]{:S(2)}, u32[]{:S(2)}) collective-permute-start(bf16[1024,256]{1,0:T(8,128)(2,1)S(1)} %all_gather.3.unit_ref), channel_id=1, source_target_pairs={{0,16},{8,120},{16,32},{24,8},{32,48},{40,24},{48,64},{56,40},{64,... | collective-permute-start | bytes 1572872 | tf_op jit(solution)/shard_map/ppermute | solution.py:217
  25.0 1.0 copy-start
  32.1 12.3 %collective-permute-start.1 = (bf16[1024,256]{1,0:T(8,128)(2,1)S(1)}, bf16[1024,256]{1,0:T(8,128)(2,1)S(1)}, u32[]{:S(2)}, u32[]{:S(2)}) collective-permute-start(bf16[1024,256]{1,0:T(8,128)(2,1)S(1)} %after.7.unit_ref.refs_0_), channel_id=1, source_target_pairs={{0,16},{8,120},{16,32},{24,8},{32,48},{40,24},{48,64},{56,40},{64,... | collective-permute-start | bytes 1572872 | tf_op jit(solution)/shard_map/ppermute | solution.py:219
  44.3 3.9 %collective-permute-start.3 = (bf16[1024,256]{1,0:T(8,128)(2,1)S(1)}, bf16[1024,256]{1,0:T(8,128)(2,1)S(1)}, u32[]{:S(2)}, u32[]{:S(2)}) collective-permute-start(bf16[1024,256]{1,0:T(8,128)(2,1)S(1)} %after.9), channel_id=1, source_target_pairs={{0,8},{8,0},{16,24},{24,16},{32,40},{40,32},{48,56},{56,48},{64,72... | collective-permute-start | bytes 1572872 | tf_op jit(solution)/shard_map/ppermute | solution.py:221
  46.3 12.3 %collective-permute-start.2 = (bf16[1024,256]{1,0:T(8,128)(2,1)S(1)}, bf16[1024,256]{1,0:T(8,128)(2,1)S(1)}, u32[]{:S(2)}, u32[]{:S(2)}) collective-permute-start(bf16[1024,256]{1,0:T(8,128)(2,1)S(1)} %after.8.unit_ref), channel_id=1, source_target_pairs={{0,16},{8,120},{16,32},{24,8},{32,48},{40,24},{48,64},{56,40},{64,... | collective-permute-start | bytes 1572872 | tf_op jit(solution)/shard_map/ppermute | solution.py:224
  51.5 9.6 %collective-permute-start.5 = (bf16[1024,256]{1,0:T(8,128)(2,1)S(1)}, bf16[1024,256]{1,0:T(8,128)(2,1)S(1)}, u32[]{:S(2)}, u32[]{:S(2)}) collective-permute-start(bf16[1024,256]{1,0:T(8,128)(2,1)S(1)} %after.11), channel_id=1, source_target_pairs={{0,8},{8,0},{16,24},{24,16},{32,40},{40,32},{48,56},{56,48},{64,72... | collective-permute-start | bytes 1572872 | tf_op jit(solution)/shard_map/ppermute | solution.py:226
  58.6 12.3 %collective-permute-start.4 = (bf16[1024,256]{1,0:T(8,128)(2,1)S(1)}, bf16[1024,256]{1,0:T(8,128)(2,1)S(1)}, u32[]{:S(2)}, u32[]{:S(2)}) collective-permute-start(bf16[1024,256]{1,0:T(8,128)(2,1)S(1)} %after.10.unit_ref), channel_id=1, source_target_pairs={{0,16},{8,120},{16,32},{24,8},{32,48},{40,24},{48,64},{56,40},{64,... | collective-permute-start | bytes 1572872 | tf_op jit(solution)/shard_map/ppermute | solution.py:224
  64.3 6.6 %collective-permute-start.6 = (bf16[1024,256]{1,0:T(8,128)(2,1)S(1)}, bf16[1024,256]{1,0:T(8,128)(2,1)S(1)}, u32[]{:S(2)}, u32[]{:S(2)}) collective-permute-start(bf16[1024,256]{1,0:T(8,128)(2,1)S(1)} %after.13), channel_id=1, source_target_pairs={{0,8},{8,0},{16,24},{24,16},{32,40},{40,32},{48,56},{56,48},{64,72... | collective-permute-start | bytes 1572872 | tf_op jit(solution)/shard_map/ppermute | solution.py:226

commit v4 on v3

--- a/solution.py
+++ b/solution.py
@@ -11,7 +11,7 @@
 HEAD_SIZE = 128
 HALF_ROWS = 64
 MASKED_SCORE = -1e30
-ROW_TILE = 256
+ROW_TILE = 512
 CHIPS_Y, CHIPS_Z, CORES = 4, 8, 2
 
 
@@ -53,7 +53,8 @@
             ahead = scores_of(tile + 1)
         old = largest[rows, :]
         new = jnp.maximum(old, jnp.max(scores, axis=1, keepdims=True))
-        weights = jnp.exp2(scores - new[:, :1]).astype(jnp.bfloat16)
+        level = jnp.concatenate([new] * (unit.shape[0] // HEAD_SIZE), axis=1)
+        weights = jnp.exp2(scores - level).astype(jnp.bfloat16)
         fade = jnp.exp2(old - new)
         product = jnp.dot(weights, values, preferred_element_type=jnp.float32)
         total[rows, :] = total[rows, :] * jnp.concatenate([fade, fade], axis=1) + product

time: 108 us -> 108 us (level)
  transfers between devices with their start and end apart: 7 -> 7, of which waited for: 3 -> 3; matrix products, arithmetic and copies ran while one was open for 4% -> 4% of each run, Pallas kernels for 18% -> 19%
where the time goes in v4:
time: 108 us; the launch traced here: 107 us
  blocking collectives  47.3 us (44%)
  Pallas kernels  26.8 us (25%)
  starting transfers between devices  16.6 us (15%)
  waiting for transfers between devices  10 us (9%)
  local copies, waits for them, and re-layouts  5.54 us (5%)
    all_to_all x1, blocking collectives, on_device(): lax.all_to_all(attended, 'tp', split_axis=0, concat_axis=1, tiled=True)  28.8 us
    pallas_call x6, Pallas kernels, attend_next(): pl.pallas_call(functools.partial(next_kernel, turn), out_shape=state, in_...  19.8 us
    all_gather x1, blocking collectives, on_device(): lax.all_gather(kv, 'seq', axis=0, tiled=True, axis_index_groups=COLUMNS)  18.5 us
    ppermute x3, starting transfers between devices, on_device(): other = lax.ppermute(after(here, largest), 'seq', OTHER_CORE)  8.36 us
    ppermute x3, waiting for transfers between devices, on_device(): unit = lax.ppermute(here, 'seq', ALONG_Z)  7.69 us
    ppermute x3, starting transfers between devices, on_device(): unit = lax.ppermute(here, 'seq', ALONG_Z)  6.35 us
    pallas_call x1, Pallas kernels, on_device(): pl.pallas_call(first_kernel, out_shape=[pltpu.VMEM((row_count, 2 * HEAD_S...  3.68 us
    pallas_call x1, Pallas kernels, on_device(): pl.pallas_call(functools.partial(last_kernel, len(distances) - 1), out_sh...  3.36 us
  transfers between devices with their start and end apart: 7, of which 3 were waited for; matrix products, arithmetic and copies ran while one was open for 4% of the time, Pallas kernels for 19%

profile of v4, /device:TPU:16, one launch (start us, length us, event | category | flops | bytes accessed | tf_op | source)
XLA Modules:
  0.0 107.5 jit_solution(10499852053570894557)
XLA Ops:
  0.0 0.8 pad_maximum_fusion
  0.8 18.5 %all_gather.3.unit_ref = bf16[1024,256]{1,0:T(8,128)(2,1)S(1)} all-gather(bf16[128,256]{1,0:T(8,128)(2,1)S(1)} %pad_maximum_fusion), channel_id=1, replica_groups={{0,8,128,136,256,264,384,392},{16,24,144,152,272,280,400,408},{32,40,16..., dimensions={0}, use_global_device_ids=true | all-gather | bytes 589824 | tf_op jit(solution)/shard_map/all_gather | solution.py:163
  19.2 1.9 %collective-permute-start = (bf16[1024,256]{1,0:T(8,128)(2,1)S(1)}, bf16[1024,256]{1,0:T(8,128)(2,1)S(1)}, u32[]{:S(2)}, u32[]{:S(2)}) collective-permute-start(bf16[1024,256]{1,0:T(8,128)(2,1)S(1)} %all_gather.3.unit_ref), channel_id=1, source_target_pairs={{0,16},{8,120},{16,32},{24,8},{32,48},{40,24},{48,64},{56,40},{64,... | collective-permute-start | bytes 1572872 | tf_op jit(solution)/shard_map/ppermute | solution.py:218
  21.2 0.8 copy.29
  22.0 0.1 reshape.195
  22.0 0.1 copy.30
  22.1 0.1 dynamic-slice_add_fusion
  22.2 0.3 slice_reduce_fusion
  22.5 0.1 broadcast_in_dim.31
  22.6 0.1 stack.20
  22.7 0.1 broadcast_in_dim.32
  22.7 0.1 stack.21
  22.8 0.1 broadcast_in_dim.33
  22.9 0.1 stack.22
  23.0 0.1 broadcast_in_dim.34
  23.0 0.1 stack.23
  23.1 0.1 broadcast_in_dim.35
  23.2 0.1 stack.24
  23.3 0.1 broadcast_in_dim.36
  23.3 0.1 stack.25
  23.4 0.1 broadcast_in_dim.37
  23.5 0.1 stack.26
  23.6 0.1 stack.28
  23.6 0.1 stack.27
  23.7 0.1 broadcast_in_dim.29
  23.8 0.1 broadcast_in_dim.30
  24.0 0.9 dynamic-slice_reduce_fusion.own_ref
  24.8 0.1 lt.44
  24.9 0.1 compare_select_fusion.bias_ref
  25.0 0.0 copy-start
  25.0 1.0 copy-done
  26.0 3.7 %attend_first.1 = (bf16[2048,256]{1,0:T(8,128)(2,1)S(1)}, f32[2048,256]{1,0:T(8,128)S(1)}, f32[2048,128]{1,0:T(8,128)S(1)}) custom-call(s32[2]{0:T(128)S(1)} %dynamic-slice_reduce_fusion.own_ref, bf16[128,2048]{1,0:T(8,128)(2,1)S(1)} %copy-done, bf16[1024,256]{1,0:T(8,128)(2,1)S(1)} %all_gather.3.unit_ref, s32[1,1024]{1,0:T(1,128)S(1)} %and_add_fusion.pos_ref, ...), custom_call_target="tpu_custom_call" | custom-call | flops 2147483648 | bytes 2097152 | tf_op jit(solution)/shard_map/attend_first/pallas_call | solution.py:196
  29.7 2.3 %collective-permute-done.refs_0_ = bf16[1024,256]{1,0:T(8,128)(2,1)S(1)} collective-permute-done((bf16[1024,256]{1,0:T(8,128)(2,1)S(1)}, bf16[1024,256]{1,0:T(8,128)(2,1)S(1)}, u32[]{:S(2)}, u32[]{:S(2)}) %collective-permute-start) | collective-permute-done | bytes 524320 | tf_op jit(solution)/shard_map/ppermute | solution.py:218
  32.1 1.9 %collective-permute-start.1 = (bf16[1024,256]{1,0:T(8,128)(2,1)S(1)}, bf16[1024,256]{1,0:T(8,128)(2,1)S(1)}, u32[]{:S(2)}, u32[]{:S(2)}) collective-permute-start(bf16[1024,256]{1,0:T(8,128)(2,1)S(1)} %after.7.unit_ref.refs_0_), channel_id=1, source_target_pairs={{0,16},{8,120},{16,32},{24,8},{32,48},{40,24},{48,64},{56,40},{64,... | collective-permute-start | bytes 1572872 | tf_op jit(solution)/shard_map/ppermute | solution.py:220
  34.0 3.3 %attend_next.6 = (f32[2048,256]{1,0:T(8,128)S(1)}, f32[2048,128]{1,0:T(8,128)S(1)}) custom-call(bf16[2048,256]{1,0:T(8,128)(2,1)S(1)} %get-tuple-element.21.scaled, bf16[1024,256]{1,0:T(8,128)(2,1)S(1)} %after.7.unit_ref.refs_0_, f32[14,1024]{1,0:T(8,128)S(1)} %compare_select_fusion.bias_ref, ...), custom_call_target="tpu_custom_call", output_to_operand_aliasing={{0}: (3, {}), {1}: (4, {})} | custom-call | flops 2147483648 | bytes 2097152 | tf_op jit(solution)/shard_map/attend_next/pallas_call | solution.py:207
  37.3 7.1 %collective-permute-done.1.refs_0_ = bf16[1024,256]{1,0:T(8,128)(2,1)S(1)} collective-permute-done((bf16[1024,256]{1,0:T(8,128)(2,1)S(1)}, bf16[1024,256]{1,0:T(8,128)(2,1)S(1)}, u32[]{:S(2)}, u32[]{:S(2)}) %collective-permute-start.1) | collective-permute-done | bytes 524320 | tf_op jit(solution)/shard_map/ppermute | solution.py:220
  44.3 1.9 %collective-permute-start.3 = (bf16[1024,256]{1,0:T(8,128)(2,1)S(1)}, bf16[1024,256]{1,0:T(8,128)(2,1)S(1)}, u32[]{:S(2)}, u32[]{:S(2)}) collective-permute-start(bf16[1024,256]{1,0:T(8,128)(2,1)S(1)} %after.9), channel_id=1, source_target_pairs={{0,8},{8,0},{16,24},{24,16},{32,40},{40,32},{48,56},{56,48},{64,72... | collective-permute-start | bytes 1572872 | tf_op jit(solution)/shard_map/ppermute | solution.py:222
  46.3 1.9 %collective-permute-start.2 = (bf16[1024,256]{1,0:T(8,128)(2,1)S(1)}, bf16[1024,256]{1,0:T(8,128)(2,1)S(1)}, u32[]{:S(2)}, u32[]{:S(2)}) collective-permute-start(bf16[1024,256]{1,0:T(8,128)(2,1)S(1)} %after.8.unit_ref), channel_id=1, source_target_pairs={{0,16},{8,120},{16,32},{24,8},{32,48},{40,24},{48,64},{56,40},{64,... | collective-permute-start | bytes 1572872 | tf_op jit(solution)/shard_map/ppermute | solution.py:225
  48.2 0.0 collective-permute-done.3.unit_ref
  48.3 3.3 %attend_next.7 = (f32[2048,256]{1,0:T(8,128)S(1)}, f32[2048,128]{1,0:T(8,128)S(1)}) custom-call(bf16[2048,256]{1,0:T(8,128)(2,1)S(1)} %get-tuple-element.21.scaled, bf16[1024,256]{1,0:T(8,128)(2,1)S(1)} %collective-permute-done.3.unit_ref, f32[14,1024]{1,0:T(8,128)S(1)} %compare_select_fusion.bias_ref, ...), custom_call_target="tpu_custom_call", output_to_operand_aliasing={{0}: (3, {}), {1}: (4, {})} | custom-call | flops 2147483648 | bytes 2097152 | tf_op jit(solution)/shard_map/attend_next/pallas_call | solution.py:207
  51.6 3.1 %collective-permute-start.5 = (bf16[1024,256]{1,0:T(8,128)(2,1)S(1)}, bf16[1024,256]{1,0:T(8,128)(2,1)S(1)}, u32[]{:S(2)}, u32[]{:S(2)}) collective-permute-start(bf16[1024,256]{1,0:T(8,128)(2,1)S(1)} %after.11), channel_id=1, source_target_pairs={{0,8},{8,0},{16,24},{24,16},{32,40},{40,32},{48,56},{56,48},{64,72... | collective-permute-start | bytes 1572872 | tf_op jit(solution)/shard_map/ppermute | solution.py:227
  54.7 3.3 %attend_next.8 = (f32[2048,256]{1,0:T(8,128)S(1)}, f32[2048,128]{1,0:T(8,128)S(1)}) custom-call(bf16[2048,256]{1,0:T(8,128)(2,1)S(1)} %get-tuple-element.21.scaled, bf16[1024,256]{1,0:T(8,128)(2,1)S(1)} %after.8.unit_ref, f32[14,1024]{1,0:T(8,128)S(1)} %compare_select_fusion.bias_ref, ...), custom_call_target="tpu_custom_call", output_to_operand_aliasing={{0}: (3, {}), {1}: (4, {})} | custom-call | flops 2147483648 | bytes 2097152 | tf_op jit(solution)/shard_map/attend_next/pallas_call | solution.py:207
  58.0 0.6 collective-permute-done.2.refs_0_
  58.6 2.5 %collective-permute-start.4 = (bf16[1024,256]{1,0:T(8,128)(2,1)S(1)}, bf16[1024,256]{1,0:T(8,128)(2,1)S(1)}, u32[]{:S(2)}, u32[]{:S(2)}) collective-permute-start(bf16[1024,256]{1,0:T(8,128)(2,1)S(1)} %after.10.unit_ref), channel_id=1, source_target_pairs={{0,16},{8,120},{16,32},{24,8},{32,48},{40,24},{48,64},{56,40},{64,... | collective-permute-start | bytes 1572872 | tf_op jit(solution)/shard_map/ppermute | solution.py:225
  61.2 0.0 collective-permute-done.5.unit_ref
  61.2 3.3 %attend_next.9 = (f32[2048,256]{1,0:T(8,128)S(1)}, f32[2048,128]{1,0:T(8,128)S(1)}) custom-call(bf16[2048,256]{1,0:T(8,128)(2,1)S(1)} %get-tuple-element.21.scaled, bf16[1024,256]{1,0:T(8,128)(2,1)S(1)} %collective-permute-done.5.unit_ref, f32[14,1024]{1,0:T(8,128)S(1)} %compare_select_fusion.bias_ref, ...), custom_call_target="tpu_custom_call", output_to_operand_aliasing={{0}: (3, {}), {1}: (4, {})} | custom-call | flops 2147483648 | bytes 2097152 | tf_op jit(solution)/shard_map/attend_next/pallas_call | solution.py:207
  64.5 3.4 %collective-permute-start.6 = (bf16[1024,256]{1,0:T(8,128)(2,1)S(1)}, bf16[1024,256]{1,0:T(8,128)(2,1)S(1)}, u32[]{:S(2)}, u32[]{:S(2)}) collective-permute-start(bf16[1024,256]{1,0:T(8,128)(2,1)S(1)} %after.13), channel_id=1, source_target_pairs={{0,8},{8,0},{16,24},{24,16},{32,40},{40,32},{48,56},{56,48},{64,72... | collective-permute-start | bytes 1572872 | tf_op jit(solution)/shard_map/ppermute | solution.py:227
  67.8 3.3 %attend_next.10 = (f32[2048,256]{1,0:T(8,128)S(1)}, f32[2048,128]{1,0:T(8,128)S(1)}) custom-call(bf16[2048,256]{1,0:T(8,128)(2,1)S(1)} %get-tuple-element.21.scaled, bf16[1024,256]{1,0:T(8,128)(2,1)S(1)} %after.10.unit_ref, f32[14,1024]{1,0:T(8,128)S(1)} %compare_select_fusion.bias_ref, ...), custom_call_target="tpu_custom_call", output_to_operand_aliasing={{0}: (3, {}), {1}: (4, {})} | custom-call | flops 2147483648 | bytes 2097152 | tf_op jit(solution)/shard_map/attend_next/pallas_call | solution.py:207
  71.2 0.0 collective-permute-done.4.refs_0_
  71.2 0.0 collective-permute-done.6.unit_ref
  71.2 3.3 %attend_next.11 = (f32[2048,256]{1,0:T(8,128)S(1)}, f32[2048,128]{1,0:T(8,128)S(1)}) custom-call(bf16[2048,256]{1,0:T(8,128)(2,1)S(1)} %get-tuple-element.21.scaled, bf16[1024,256]{1,0:T(8,128)(2,1)S(1)} %collective-permute-done.6.unit_ref, f32[14,1024]{1,0:T(8,128)S(1)} %compare_select_fusion.bias_ref, ...), custom_call_target="tpu_custom_call", output_to_operand_aliasing={{0}: (3, {}), {1}: (4, {})} | custom-call | flops 2147483648 | bytes 2097152 | tf_op jit(solution)/shard_map/attend_next/pallas_call | solution.py:207
  74.5 3.4 %attend_last.1 = (bf16[128,2048]{1,0:T(8,128)(2,1)S(1)}, f32[2048,256]{1,0:T(8,128)S(1)}, f32[2048,128]{1,0:T(8,128)S(1)}) custom-call(bf16[2048,256]{1,0:T(8,128)(2,1)S(1)} %get-tuple-element.21.scaled, bf16[1024,256]{1,0:T(8,128)(2,1)S(1)} %after.12.unit_ref, ...), custom_call_target="tpu_custom_call", output_to_operand_aliasing={{1}: (3, {}), {2}: (4, {})} | custom-call | flops 2147483648 | bytes 2097152 | tf_op jit(solution)/shard_map/attend_last/pallas_call | solution.py:231
  77.8 28.8 %all_to_all.19 = bf16[8,16,2048]{2,1,0:T(8,128)(2,1)S(1)} all-to-all(bf16[8,16,2048]{2,1,0:T(8,128)(2,1)S(1)} %bitcast.6), channel_id=1, replica_groups=mesh['seq'=64,'tp'=8] {'tp'}, dimensions={0} | all-to-all | bytes 1048576 | tf_op jit(solution)/shard_map/all_to_all | solution.py:241
  106.7 0.8 copy.32
  (14 shorter events, 0.2 us)
Async XLA Ops:
  19.2 12.8 %collective-permute-start = (bf16[1024,256]{1,0:T(8,128)(2,1)S(1)}, bf16[1024,256]{1,0:T(8,128)(2,1)S(1)}, u32[]{:S(2)}, u32[]{:S(2)}) collective-permute-start(bf16[1024,256]{1,0:T(8,128)(2,1)S(1)} %all_gather.3.unit_ref), channel_id=1, source_target_pairs={{0,16},{8,120},{16,32},{24,8},{32,48},{40,24},{48,64},{56,40},{64,... | collective-permute-start | bytes 1572872 | tf_op jit(solution)/shard_map/ppermute | solution.py:218
  25.0 1.0 copy-start
  32.1 12.3 %collective-permute-start.1 = (bf16[1024,256]{1,0:T(8,128)(2,1)S(1)}, bf16[1024,256]{1,0:T(8,128)(2,1)S(1)}, u32[]{:S(2)}, u32[]{:S(2)}) collective-permute-start(bf16[1024,256]{1,0:T(8,128)(2,1)S(1)} %after.7.unit_ref.refs_0_), channel_id=1, source_target_pairs={{0,16},{8,120},{16,32},{24,8},{32,48},{40,24},{48,64},{56,40},{64,... | collective-permute-start | bytes 1572872 | tf_op jit(solution)/shard_map/ppermute | solution.py:220
  44.3 3.9 %collective-permute-start.3 = (bf16[1024,256]{1,0:T(8,128)(2,1)S(1)}, bf16[1024,256]{1,0:T(8,128)(2,1)S(1)}, u32[]{:S(2)}, u32[]{:S(2)}) collective-permute-start(bf16[1024,256]{1,0:T(8,128)(2,1)S(1)} %after.9), channel_id=1, source_target_pairs={{0,8},{8,0},{16,24},{24,16},{32,40},{40,32},{48,56},{56,48},{64,72... | collective-permute-start | bytes 1572872 | tf_op jit(solution)/shard_map/ppermute | solution.py:222
  46.3 12.3 %collective-permute-start.2 = (bf16[1024,256]{1,0:T(8,128)(2,1)S(1)}, bf16[1024,256]{1,0:T(8,128)(2,1)S(1)}, u32[]{:S(2)}, u32[]{:S(2)}) collective-permute-start(bf16[1024,256]{1,0:T(8,128)(2,1)S(1)} %after.8.unit_ref), channel_id=1, source_target_pairs={{0,16},{8,120},{16,32},{24,8},{32,48},{40,24},{48,64},{56,40},{64,... | collective-permute-start | bytes 1572872 | tf_op jit(solution)/shard_map/ppermute | solution.py:225
  51.6 9.6 %collective-permute-start.5 = (bf16[1024,256]{1,0:T(8,128)(2,1)S(1)}, bf16[1024,256]{1,0:T(8,128)(2,1)S(1)}, u32[]{:S(2)}, u32[]{:S(2)}) collective-permute-start(bf16[1024,256]{1,0:T(8,128)(2,1)S(1)} %after.11), channel_id=1, source_target_pairs={{0,8},{8,0},{16,24},{24,16},{32,40},{40,32},{48,56},{56,48},{64,72... | collective-permute-start | bytes 1572872 | tf_op jit(solution)/shard_map/ppermute | solution.py:227
  58.6 12.5 %collective-permute-start.4 = (bf16[1024,256]{1,0:T(8,128)(2,1)S(1)}, bf16[1024,256]{1,0:T(8,128)(2,1)S(1)}, u32[]{:S(2)}, u32[]{:S(2)}) collective-permute-start(bf16[1024,256]{1,0:T(8,128)(2,1)S(1)} %after.10.unit_ref), channel_id=1, source_target_pairs={{0,16},{8,120},{16,32},{24,8},{32,48},{40,24},{48,64},{56,40},{64,... | collective-permute-start | bytes 1572872 | tf_op jit(solution)/shard_map/ppermute | solution.py:225
  64.5 6.7 %collective-permute-start.6 = (bf16[1024,256]{1,0:T(8,128)(2,1)S(1)}, bf16[1024,256]{1,0:T(8,128)(2,1)S(1)}, u32[]{:S(2)}, u32[]{:S(2)}) collective-permute-start(bf16[1024,256]{1,0:T(8,128)(2,1)S(1)} %after.13), channel_id=1, source_target_pairs={{0,8},{8,0},{16,24},{24,16},{32,40},{40,32},{48,56},{56,48},{64,72... | collective-permute-start | bytes 1572872 | tf_op jit(solution)/shard_map/ppermute | solution.py:227

commit v5 on v4

--- a/solution.py
+++ b/solution.py
@@ -11,7 +11,7 @@
 HEAD_SIZE = 128
 HALF_ROWS = 64
 MASKED_SCORE = -1e30
-ROW_TILE = 512
+ROW_TILE = 256
 CHIPS_Y, CHIPS_Z, CORES = 4, 8, 2
 
 

time: 108 us -> 106 us (0.981)
  Pallas kernels: 26.8 us -> 24.2 us
  waiting for transfers between devices: 10 us -> 12.3 us
  blocking collectives: 47.3 us -> 46.1 us
    ppermute x3, waiting for transfers between devices: 7.69 us -> 9.87 us  [on_device(): unit = lax.ppermute(here, 'seq', ALONG_Z)]
    pallas_call x6, Pallas kernels: 19.8 us -> 17.7 us  [attend_next(): pl.pallas_call(functools.partial(next_kernel, turn), out_shape=state, in_...]
    all_to_all x1, blocking collectives: 28.8 us -> 27.7 us  [on_device(): lax.all_to_all(attended, 'tp', split_axis=0, concat_axis=1, tiled=True)]
  transfers between devices with their start and end apart: 7 -> 7, of which waited for: 3 -> 4; matrix products, arithmetic and copies ran while one was open for 4% -> 4% of each run, Pallas kernels for 19% -> 17%
where the time goes in v5:
time: 106 us; the launch traced here: 105 us
  blocking collectives  46.1 us (43%)
  Pallas kernels  24.2 us (23%)
  starting transfers between devices  15.9 us (15%)
  waiting for transfers between devices  12.3 us (12%)
  local copies, waits for them, and re-layouts  5.54 us (5%)
    all_to_all x1, blocking collectives, on_device(): lax.all_to_all(attended, 'tp', split_axis=0, concat_axis=1, tiled=True)  27.7 us
    all_gather x1, blocking collectives, on_device(): lax.all_gather(kv, 'seq', axis=0, tiled=True, axis_index_groups=COLUMNS)  18.5 us
    pallas_call x6, Pallas kernels, attend_next(): pl.pallas_call(functools.partial(next_kernel, turn), out_shape=state, in_...  17.7 us
    ppermute x3, waiting for transfers between devices, on_device(): unit = lax.ppermute(here, 'seq', ALONG_Z)  9.87 us
    ppermute x3, starting transfers between devices, on_device(): other = lax.ppermute(after(here, largest), 'seq', OTHER_CORE)  8.27 us
    ppermute x3, starting transfers between devices, on_device(): unit = lax.ppermute(here, 'seq', ALONG_Z)  5.75 us
    pallas_call x1, Pallas kernels, on_device(): pl.pallas_call(first_kernel, out_shape=[pltpu.VMEM((row_count, 2 * HEAD_S...  3.56 us
    pallas_call x1, Pallas kernels, on_device(): pl.pallas_call(functools.partial(last_kernel, len(distances) - 1), out_sh...  2.97 us
  transfers between devices with their start and end apart: 7, of which 4 were waited for; matrix products, arithmetic and copies ran while one was open for 4% of the time, Pallas kernels for 17%

profile of v5, /device:TPU:16, one launch (start us, length us, event | category | flops | bytes accessed | tf_op | source)
XLA Modules:
  0.0 105.4 jit_solution(18001305374613555183)
XLA Ops:
  0.0 0.8 pad_maximum_fusion
  0.8 18.5 %all_gather.3.unit_ref = bf16[1024,256]{1,0:T(8,128)(2,1)S(1)} all-gather(bf16[128,256]{1,0:T(8,128)(2,1)S(1)} %pad_maximum_fusion), channel_id=1, replica_groups={{0,8,128,136,256,264,384,392},{16,24,144,152,272,280,400,408},{32,40,16..., dimensions={0}, use_global_device_ids=true | all-gather | bytes 589824 | tf_op jit(solution)/shard_map/all_gather | solution.py:163
  19.2 1.9 %collective-permute-start = (bf16[1024,256]{1,0:T(8,128)(2,1)S(1)}, bf16[1024,256]{1,0:T(8,128)(2,1)S(1)}, u32[]{:S(2)}, u32[]{:S(2)}) collective-permute-start(bf16[1024,256]{1,0:T(8,128)(2,1)S(1)} %all_gather.3.unit_ref), channel_id=1, source_target_pairs={{0,16},{8,120},{16,32},{24,8},{32,48},{40,24},{48,64},{56,40},{64,... | collective-permute-start | bytes 1572872 | tf_op jit(solution)/shard_map/ppermute | solution.py:218
  21.2 0.8 copy.29
  22.0 0.1 reshape.195
  22.0 0.1 copy.30
  22.1 0.1 dynamic-slice_add_fusion
  22.2 0.3 slice_reduce_fusion
  22.5 0.1 broadcast_in_dim.31
  22.6 0.1 stack.20
  22.7 0.1 broadcast_in_dim.32
  22.7 0.1 stack.21
  22.8 0.1 broadcast_in_dim.33
  22.9 0.1 stack.22
  23.0 0.1 broadcast_in_dim.34
  23.0 0.1 stack.23
  23.1 0.1 broadcast_in_dim.35
  23.2 0.1 stack.24
  23.3 0.1 broadcast_in_dim.36
  23.3 0.1 stack.25
  23.4 0.1 broadcast_in_dim.37
  23.5 0.1 stack.26
  23.6 0.1 stack.28
  23.6 0.1 stack.27
  23.7 0.1 broadcast_in_dim.29
  23.8 0.1 broadcast_in_dim.30
  24.0 0.9 dynamic-slice_reduce_fusion.own_ref
  24.8 0.1 lt.44
  24.9 0.1 compare_select_fusion.bias_ref
  25.0 0.0 copy-start
  25.0 1.0 copy-done
  26.0 3.6 %attend_first.1 = (bf16[2048,256]{1,0:T(8,128)(2,1)S(1)}, f32[2048,256]{1,0:T(8,128)S(1)}, f32[2048,128]{1,0:T(8,128)S(1)}) custom-call(s32[2]{0:T(128)S(1)} %dynamic-slice_reduce_fusion.own_ref, bf16[128,2048]{1,0:T(8,128)(2,1)S(1)} %copy-done, bf16[1024,256]{1,0:T(8,128)(2,1)S(1)} %all_gather.3.unit_ref, s32[1,1024]{1,0:T(1,128)S(1)} %and_add_fusion.pos_ref, ...), custom_call_target="tpu_custom_call" | custom-call | flops 2147483648 | bytes 2097152 | tf_op jit(solution)/shard_map/attend_first/pallas_call | solution.py:196
  29.6 2.5 %collective-permute-done.refs_0_ = bf16[1024,256]{1,0:T(8,128)(2,1)S(1)} collective-permute-done((bf16[1024,256]{1,0:T(8,128)(2,1)S(1)}, bf16[1024,256]{1,0:T(8,128)(2,1)S(1)}, u32[]{:S(2)}, u32[]{:S(2)}) %collective-permute-start) | collective-permute-done | bytes 524320 | tf_op jit(solution)/shard_map/ppermute | solution.py:218
  32.1 1.9 %collective-permute-start.1 = (bf16[1024,256]{1,0:T(8,128)(2,1)S(1)}, bf16[1024,256]{1,0:T(8,128)(2,1)S(1)}, u32[]{:S(2)}, u32[]{:S(2)}) collective-permute-start(bf16[1024,256]{1,0:T(8,128)(2,1)S(1)} %after.7.unit_ref.refs_0_), channel_id=1, source_target_pairs={{0,16},{8,120},{16,32},{24,8},{32,48},{40,24},{48,64},{56,40},{64,... | collective-permute-start | bytes 1572872 | tf_op jit(solution)/shard_map/ppermute | solution.py:220
  34.0 3.0 %attend_next.6 = (f32[2048,256]{1,0:T(8,128)S(1)}, f32[2048,128]{1,0:T(8,128)S(1)}) custom-call(bf16[2048,256]{1,0:T(8,128)(2,1)S(1)} %get-tuple-element.21.scaled, bf16[1024,256]{1,0:T(8,128)(2,1)S(1)} %after.7.unit_ref.refs_0_, f32[14,1024]{1,0:T(8,128)S(1)} %compare_select_fusion.bias_ref, ...), custom_call_target="tpu_custom_call", output_to_operand_aliasing={{0}: (3, {}), {1}: (4, {})} | custom-call | flops 2147483648 | bytes 2097152 | tf_op jit(solution)/shard_map/attend_next/pallas_call | solution.py:207
  36.9 7.4 %collective-permute-done.1.refs_0_ = bf16[1024,256]{1,0:T(8,128)(2,1)S(1)} collective-permute-done((bf16[1024,256]{1,0:T(8,128)(2,1)S(1)}, bf16[1024,256]{1,0:T(8,128)(2,1)S(1)}, u32[]{:S(2)}, u32[]{:S(2)}) %collective-permute-start.1) | collective-permute-done | bytes 524320 | tf_op jit(solution)/shard_map/ppermute | solution.py:220
  44.3 1.9 %collective-permute-start.3 = (bf16[1024,256]{1,0:T(8,128)(2,1)S(1)}, bf16[1024,256]{1,0:T(8,128)(2,1)S(1)}, u32[]{:S(2)}, u32[]{:S(2)}) collective-permute-start(bf16[1024,256]{1,0:T(8,128)(2,1)S(1)} %after.9), channel_id=1, source_target_pairs={{0,8},{8,0},{16,24},{24,16},{32,40},{40,32},{48,56},{56,48},{64,72... | collective-permute-start | bytes 1572872 | tf_op jit(solution)/shard_map/ppermute | solution.py:222
  46.3 1.9 %collective-permute-start.2 = (bf16[1024,256]{1,0:T(8,128)(2,1)S(1)}, bf16[1024,256]{1,0:T(8,128)(2,1)S(1)}, u32[]{:S(2)}, u32[]{:S(2)}) collective-permute-start(bf16[1024,256]{1,0:T(8,128)(2,1)S(1)} %after.8.unit_ref), channel_id=1, source_target_pairs={{0,16},{8,120},{16,32},{24,8},{32,48},{40,24},{48,64},{56,40},{64,... | collective-permute-start | bytes 1572872 | tf_op jit(solution)/shard_map/ppermute | solution.py:225
  48.2 0.0 collective-permute-done.3.unit_ref
  48.3 2.9 %attend_next.7 = (f32[2048,256]{1,0:T(8,128)S(1)}, f32[2048,128]{1,0:T(8,128)S(1)}) custom-call(bf16[2048,256]{1,0:T(8,128)(2,1)S(1)} %get-tuple-element.21.scaled, bf16[1024,256]{1,0:T(8,128)(2,1)S(1)} %collective-permute-done.3.unit_ref, f32[14,1024]{1,0:T(8,128)S(1)} %compare_select_fusion.bias_ref, ...), custom_call_target="tpu_custom_call", output_to_operand_aliasing={{0}: (3, {}), {1}: (4, {})} | custom-call | flops 2147483648 | bytes 2097152 | tf_op jit(solution)/shard_map/attend_next/pallas_call | solution.py:207
  51.2 3.1 %collective-permute-start.5 = (bf16[1024,256]{1,0:T(8,128)(2,1)S(1)}, bf16[1024,256]{1,0:T(8,128)(2,1)S(1)}, u32[]{:S(2)}, u32[]{:S(2)}) collective-permute-start(bf16[1024,256]{1,0:T(8,128)(2,1)S(1)} %after.11), channel_id=1, source_target_pairs={{0,8},{8,0},{16,24},{24,16},{32,40},{40,32},{48,56},{56,48},{64,72... | collective-permute-start | bytes 1572872 | tf_op jit(solution)/shard_map/ppermute | solution.py:227
  54.3 2.9 %attend_next.8 = (f32[2048,256]{1,0:T(8,128)S(1)}, f32[2048,128]{1,0:T(8,128)S(1)}) custom-call(bf16[2048,256]{1,0:T(8,128)(2,1)S(1)} %get-tuple-element.21.scaled, bf16[1024,256]{1,0:T(8,128)(2,1)S(1)} %after.8.unit_ref, f32[14,1024]{1,0:T(8,128)S(1)} %compare_select_fusion.bias_ref, ...), custom_call_target="tpu_custom_call", output_to_operand_aliasing={{0}: (3, {}), {1}: (4, {})} | custom-call | flops 2147483648 | bytes 2097152 | tf_op jit(solution)/shard_map/attend_next/pallas_call | solution.py:207
  57.3 1.3 %collective-permute-done.2.refs_0_ = bf16[1024,256]{1,0:T(8,128)(2,1)S(1)} collective-permute-done((bf16[1024,256]{1,0:T(8,128)(2,1)S(1)}, bf16[1024,256]{1,0:T(8,128)(2,1)S(1)}, u32[]{:S(2)}, u32[]{:S(2)}) %collective-permute-start.2) | collective-permute-done | bytes 524320 | tf_op jit(solution)/shard_map/ppermute | solution.py:225
  58.6 1.9 %collective-permute-start.4 = (bf16[1024,256]{1,0:T(8,128)(2,1)S(1)}, bf16[1024,256]{1,0:T(8,128)(2,1)S(1)}, u32[]{:S(2)}, u32[]{:S(2)}) collective-permute-start(bf16[1024,256]{1,0:T(8,128)(2,1)S(1)} %after.10.unit_ref), channel_id=1, source_target_pairs={{0,16},{8,120},{16,32},{24,8},{32,48},{40,24},{48,64},{56,40},{64,... | collective-permute-start | bytes 1572872 | tf_op jit(solution)/shard_map/ppermute | solution.py:225
  60.6 0.0 collective-permute-done.5.unit_ref
  60.6 2.9 %attend_next.9 = (f32[2048,256]{1,0:T(8,128)S(1)}, f32[2048,128]{1,0:T(8,128)S(1)}) custom-call(bf16[2048,256]{1,0:T(8,128)(2,1)S(1)} %get-tuple-element.21.scaled, bf16[1024,256]{1,0:T(8,128)(2,1)S(1)} %collective-permute-done.5.unit_ref, f32[14,1024]{1,0:T(8,128)S(1)} %compare_select_fusion.bias_ref, ...), custom_call_target="tpu_custom_call", output_to_operand_aliasing={{0}: (3, {}), {1}: (4, {})} | custom-call | flops 2147483648 | bytes 2097152 | tf_op jit(solution)/shard_map/attend_next/pallas_call | solution.py:207
  63.5 3.3 %collective-permute-start.6 = (bf16[1024,256]{1,0:T(8,128)(2,1)S(1)}, bf16[1024,256]{1,0:T(8,128)(2,1)S(1)}, u32[]{:S(2)}, u32[]{:S(2)}) collective-permute-start(bf16[1024,256]{1,0:T(8,128)(2,1)S(1)} %after.13), channel_id=1, source_target_pairs={{0,8},{8,0},{16,24},{24,16},{32,40},{40,32},{48,56},{56,48},{64,72... | collective-permute-start | bytes 1572872 | tf_op jit(solution)/shard_map/ppermute | solution.py:227
  66.8 2.9 %attend_next.10 = (f32[2048,256]{1,0:T(8,128)S(1)}, f32[2048,128]{1,0:T(8,128)S(1)}) custom-call(bf16[2048,256]{1,0:T(8,128)(2,1)S(1)} %get-tuple-element.21.scaled, bf16[1024,256]{1,0:T(8,128)(2,1)S(1)} %after.10.unit_ref, f32[14,1024]{1,0:T(8,128)S(1)} %compare_select_fusion.bias_ref, ...), custom_call_target="tpu_custom_call", output_to_operand_aliasing={{0}: (3, {}), {1}: (4, {})} | custom-call | flops 2147483648 | bytes 2097152 | tf_op jit(solution)/shard_map/attend_next/pallas_call | solution.py:207
  69.8 1.1 %collective-permute-done.4.refs_0_ = bf16[1024,256]{1,0:T(8,128)(2,1)S(1)} collective-permute-done((bf16[1024,256]{1,0:T(8,128)(2,1)S(1)}, bf16[1024,256]{1,0:T(8,128)(2,1)S(1)}, u32[]{:S(2)}, u32[]{:S(2)}) %collective-permute-start.4) | collective-permute-done | bytes 524320 | tf_op jit(solution)/shard_map/ppermute | solution.py:225
  70.9 0.0 collective-permute-done.6.unit_ref
  70.9 2.9 %attend_next.11 = (f32[2048,256]{1,0:T(8,128)S(1)}, f32[2048,128]{1,0:T(8,128)S(1)}) custom-call(bf16[2048,256]{1,0:T(8,128)(2,1)S(1)} %get-tuple-element.21.scaled, bf16[1024,256]{1,0:T(8,128)(2,1)S(1)} %collective-permute-done.6.unit_ref, f32[14,1024]{1,0:T(8,128)S(1)} %compare_select_fusion.bias_ref, ...), custom_call_target="tpu_custom_call", output_to_operand_aliasing={{0}: (3, {}), {1}: (4, {})} | custom-call | flops 2147483648 | bytes 2097152 | tf_op jit(solution)/shard_map/attend_next/pallas_call | solution.py:207
  73.9 3.0 %attend_last.1 = (bf16[128,2048]{1,0:T(8,128)(2,1)S(1)}, f32[2048,256]{1,0:T(8,128)S(1)}, f32[2048,128]{1,0:T(8,128)S(1)}) custom-call(bf16[2048,256]{1,0:T(8,128)(2,1)S(1)} %get-tuple-element.21.scaled, bf16[1024,256]{1,0:T(8,128)(2,1)S(1)} %after.12.unit_ref, ...), custom_call_target="tpu_custom_call", output_to_operand_aliasing={{1}: (3, {}), {2}: (4, {})} | custom-call | flops 2147483648 | bytes 2097152 | tf_op jit(solution)/shard_map/attend_last/pallas_call | solution.py:231
  76.9 27.7 %all_to_all.19 = bf16[8,16,2048]{2,1,0:T(8,128)(2,1)S(1)} all-to-all(bf16[8,16,2048]{2,1,0:T(8,128)(2,1)S(1)} %bitcast.6), channel_id=1, replica_groups=mesh['seq'=64,'tp'=8] {'tp'}, dimensions={0} | all-to-all | bytes 1048576 | tf_op jit(solution)/shard_map/all_to_all | solution.py:241
  104.5 0.8 copy.32
  (14 shorter events, 0.2 us)
Async XLA Ops:
  19.2 12.8 %collective-permute-start = (bf16[1024,256]{1,0:T(8,128)(2,1)S(1)}, bf16[1024,256]{1,0:T(8,128)(2,1)S(1)}, u32[]{:S(2)}, u32[]{:S(2)}) collective-permute-start(bf16[1024,256]{1,0:T(8,128)(2,1)S(1)} %all_gather.3.unit_ref), channel_id=1, source_target_pairs={{0,16},{8,120},{16,32},{24,8},{32,48},{40,24},{48,64},{56,40},{64,... | collective-permute-start | bytes 1572872 | tf_op jit(solution)/shard_map/ppermute | solution.py:218
  25.0 1.0 copy-start
  32.1 12.3 %collective-permute-start.1 = (bf16[1024,256]{1,0:T(8,128)(2,1)S(1)}, bf16[1024,256]{1,0:T(8,128)(2,1)S(1)}, u32[]{:S(2)}, u32[]{:S(2)}) collective-permute-start(bf16[1024,256]{1,0:T(8,128)(2,1)S(1)} %after.7.unit_ref.refs_0_), channel_id=1, source_target_pairs={{0,16},{8,120},{16,32},{24,8},{32,48},{40,24},{48,64},{56,40},{64,... | collective-permute-start | bytes 1572872 | tf_op jit(solution)/shard_map/ppermute | solution.py:220
  44.3 3.9 %collective-permute-start.3 = (bf16[1024,256]{1,0:T(8,128)(2,1)S(1)}, bf16[1024,256]{1,0:T(8,128)(2,1)S(1)}, u32[]{:S(2)}, u32[]{:S(2)}) collective-permute-start(bf16[1024,256]{1,0:T(8,128)(2,1)S(1)} %after.9), channel_id=1, source_target_pairs={{0,8},{8,0},{16,24},{24,16},{32,40},{40,32},{48,56},{56,48},{64,72... | collective-permute-start | bytes 1572872 | tf_op jit(solution)/shard_map/ppermute | solution.py:222
  46.3 12.3 %collective-permute-start.2 = (bf16[1024,256]{1,0:T(8,128)(2,1)S(1)}, bf16[1024,256]{1,0:T(8,128)(2,1)S(1)}, u32[]{:S(2)}, u32[]{:S(2)}) collective-permute-start(bf16[1024,256]{1,0:T(8,128)(2,1)S(1)} %after.8.unit_ref), channel_id=1, source_target_pairs={{0,16},{8,120},{16,32},{24,8},{32,48},{40,24},{48,64},{56,40},{64,... | collective-permute-start | bytes 1572872 | tf_op jit(solution)/shard_map/ppermute | solution.py:225
  51.2 9.4 %collective-permute-start.5 = (bf16[1024,256]{1,0:T(8,128)(2,1)S(1)}, bf16[1024,256]{1,0:T(8,128)(2,1)S(1)}, u32[]{:S(2)}, u32[]{:S(2)}) collective-permute-start(bf16[1024,256]{1,0:T(8,128)(2,1)S(1)} %after.11), channel_id=1, source_target_pairs={{0,8},{8,0},{16,24},{24,16},{32,40},{40,32},{48,56},{56,48},{64,72... | collective-permute-start | bytes 1572872 | tf_op jit(solution)/shard_map/ppermute | solution.py:227
  58.6 12.3 %collective-permute-start.4 = (bf16[1024,256]{1,0:T(8,128)(2,1)S(1)}, bf16[1024,256]{1,0:T(8,128)(2,1)S(1)}, u32[]{:S(2)}, u32[]{:S(2)}) collective-permute-start(bf16[1024,256]{1,0:T(8,128)(2,1)S(1)} %after.10.unit_ref), channel_id=1, source_target_pairs={{0,16},{8,120},{16,32},{24,8},{32,48},{40,24},{48,64},{56,40},{64,... | collective-permute-start | bytes 1572872 | tf_op jit(solution)/shard_map/ppermute | solution.py:225
  63.5 7.4 %collective-permute-start.6 = (bf16[1024,256]{1,0:T(8,128)(2,1)S(1)}, bf16[1024,256]{1,0:T(8,128)(2,1)S(1)}, u32[]{:S(2)}, u32[]{:S(2)}) collective-permute-start(bf16[1024,256]{1,0:T(8,128)(2,1)S(1)} %after.13), channel_id=1, source_target_pairs={{0,8},{8,0},{16,24},{24,16},{32,40},{40,32},{48,56},{56,48},{64,72... | collective-permute-start | bytes 1572872 | tf_op jit(solution)/shard_map/ppermute | solution.py:227
